TPU v7x, 256 devices: a whole 4x4x8 slice. The times are simulated.
256 devices in a mesh: dp: 32 (over y, z), tensor: 8 (over x, core).
Axes of the slice: x: 4, y: 4, z: 8, core: 2. Of those that a mesh axis runs over, the one named last changes fastest.
Arguments:
- momentum: float32 [8192, 14336], P('dp', 'tensor'), may hold values from -6 to 6
- gradient: bfloat16 [8192, 14336], P('dp', 'tensor'), may hold values from -120 to 120
- factor: bfloat16 [14336, 512], P('tensor'), may hold values from -6 to 6
- weight: bfloat16 [8192, 14336], P('dp', 'tensor'), may hold values from -6 to 6
Outputs:
- new_momentum: float32 [8192, 14336], P('dp', 'tensor')
- new_factor: bfloat16 [14336, 512], P('tensor')
- new_weight: bfloat16 [8192, 14336], P('dp', 'tensor')
All inputs are finite; a program needn't handle non-finite values.
Results may differ from a plain program's by a relative error of at most 0.0027.
Values may be sent and summed in bfloat16 or wider, within the bound.
No kernel may reach another device: no remote copies, remote signals or barrier semaphores. Data moves between devices by JAX's collectives and lax.ppermute only.
A program may use at most 64 MiB of HBM per device.

v0:
```python
import functools

import jax
import jax.numpy as jnp
from jax import lax
from jax.experimental import pallas as pl
from jax.experimental.pallas import tpu as pltpu
from jax.sharding import PartitionSpec as P

D = 8192
RANK = 512
BLOCK = 128
BLOCKS = RANK // BLOCK
UPPER = [(i, j) for i in range(BLOCKS) for j in range(i, BLOCKS)]
NY, NZ, NX = 4, 8, 4

precise = lax.Precision.HIGHEST
decay_rate = 0.95
learn_rate = 0.5
epsilon = 1e-06
f32 = jnp.float32
bf16 = jnp.bfloat16

WIDE = 896
VMEM_LIMIT = 20 * 1024 * 1024
VMEM_ALL = 60 * 1024 * 1024

Y_GROUPS = [[y * NZ + z for y in range(NY)] for z in range(NZ)]
Z_GROUPS = [[y * NZ + z for z in range(NZ)] for y in range(NY)]


def from_y(k):
    return [((i + NZ * k) % (NY * NZ), i) for i in range(NY * NZ)]


def from_z(k):
    return [(i // NZ * NZ + (i + k) % NZ, i) for i in range(NY * NZ)]


def from_x(k):
    return [((i + 2 * k) % (2 * NX), i) for i in range(2 * NX)]


def to_neighbour(odd):
    return [(i, i // NZ * NZ + ((i % NZ + odd ^ 1) - odd) % NZ) for i in range(NY * NZ)]


OTHER_CORE = [(i ^ 1, i) for i in range(2 * NX)]


def sublane(v, i):
    return jnp.broadcast_to(v[i : i + 1, :], (8, BLOCK))


def column(v, c):
    return jnp.broadcast_to(v[:, c : c + 1], (8, BLOCK))


def invert_factor(a):
    lane = lax.broadcasted_iota(jnp.int32, (8, BLOCK), 1)
    sub = lax.broadcasted_iota(jnp.int32, (8, BLOCK), 0)
    out = []
    for p in range(16):
        r = a[p]
        here = (lane >= 8 * p) & (lane < 8 * p + 8)
        cols = [column(r, 8 * p + k) for k in range(8)]
        r = jnp.where(here, jnp.where(lane == sub + 8 * p, 1.0, 0.0), r)
        x = jnp.zeros((8, BLOCK), f32)
        for j in range(8):
            pivot_col = cols[j]
            pivot = sublane(pivot_col, j)
            recip = 1.0 / pivot
            at = sub == j

            def eliminate(v, pivot_col=pivot_col, recip=recip, at=at, j=j):
                row = sublane(v, j) * recip
                return jnp.where(at, row, v - pivot_col * row)

            for k in range(j + 1, 8):
                cols[k] = eliminate(cols[k])
            x = jnp.where(at, sublane(r, j) * lax.rsqrt(pivot), x)
            r = eliminate(r)
        out.append(jnp.where(lane <= sub + 8 * p, x, 0.0))
        rows = [sublane(r, j) for j in range(8)]
        for q in range(p + 1, 16):
            v = a[q]
            t = [column(v, 8 * p + j) * rows[j] for j in range(8)]
            total = ((t[0] + t[1]) + (t[2] + t[3])) + ((t[4] + t[5]) + (t[6] + t[7]))
            a[q] = jnp.where(here, 0.0, v) - total
    return out


def cholesky_kernel(mine_ref, other_ref, after, x_ref, z_ref, g_ref, t_ref):
    few = mine_ref.shape[0]
    core = core_index()
    g_ref[pl.ds(pl.multiple_of(core * few, few), few), :] = mine_ref[...]
    g_ref[pl.ds(pl.multiple_of((1 - core) * few, few), few), :] = other_ref[...]
    for n, (i, j) in enumerate(UPPER):
        z_ref[i * BLOCK : (i + 1) * BLOCK, j * BLOCK : (j + 1) * BLOCK] = g_ref[n * BLOCK : (n + 1) * BLOCK, :]

    def spread_block(b):
        start, end = b * BLOCK, (b + 1) * BLOCK
        t = t_ref[...]
        x_ref[start:end, start:end] = t
        if b > 0:
            x_ref[start:end, :start] = dot(t, z_ref[start:end, :start])
        if b < BLOCKS - 1:
            x_ref[start:end, end:] = jnp.zeros((BLOCK, RANK - end), f32)
            u = dot(t, z_ref[start:end, end:])
            lower = dot_0(u, x_ref[start:end, :end])
            if b > 0:
                z_ref[end:, :start] = z_ref[end:, :start] - lower[:, :start]
            z_ref[end:, start:end] = -lower[:, start:]
            for i in range(b + 1, BLOCKS):
                rows = slice(i * BLOCK, (i + 1) * BLOCK)
                own = u[:, i * BLOCK - end : (i + 1) * BLOCK - end]
                z_ref[rows, i * BLOCK :] = z_ref[rows, i * BLOCK :] - dot_0(own, u[:, i * BLOCK - end :])

    def step(b, carry):
        start = pl.multiple_of(b * BLOCK, BLOCK)
        a = [z_ref[pl.ds(pl.multiple_of(start + 8 * i, 8), 8), pl.ds(start, BLOCK)] for i in range(16)]
        for i, v in enumerate(invert_factor(a)):
            t_ref[8 * i : 8 * i + 8, :] = v
        for c in range(BLOCKS):
            pl.when(b == c)(functools.partial(spread_block, c))
        return carry

    lax.fori_loop(0, BLOCKS, step, 0)


def inverse_cholesky(mine, other, after):
    return call(
        cholesky_kernel,
        [shape((RANK, RANK))],
        [VMEM, VMEM, pl.BlockSpec(memory_space=pl.ANY)],
        [
            pltpu.VMEM((RANK, RANK), f32),
            pltpu.VMEM((len(UPPER) * BLOCK, BLOCK), f32),
            pltpu.VMEM((BLOCK, BLOCK), f32),
        ],
        80 * RANK**3,
        8 * RANK**2,
    )(mine, other, after)[0]


VMEM = pl.BlockSpec(memory_space=pltpu.VMEM)


def core_index():
    return lax.rem(lax.axis_index("tensor"), 2)


def y_index():
    return lax.axis_index("dp") // NZ


def z_index():
    return lax.rem(lax.axis_index("dp"), NZ)


def shape(dims, dtype=f32):
    return jax.ShapeDtypeStruct(dims, dtype)


def dot(a, b):
    return jnp.dot(a, b, precision=precise, preferred_element_type=f32)


def dot_t(a, b):
    return lax.dot_general(a, b, (((1,), (1,)), ((), ())), precision=precise, preferred_element_type=f32)


def dot_0(a, b):
    return lax.dot_general(a, b, (((0,), (0,)), ((), ())), precision=precise, preferred_element_type=f32)


def split3(a):
    hi = a.astype(bf16)
    rest = a - hi.astype(f32)
    mid = rest.astype(bf16)
    return hi, mid, (rest - mid.astype(f32)).astype(bf16)


def call(kernel, outs, ins, scratch, flops, moved):
    return pl.pallas_call(
        kernel,
        out_shape=outs,
        in_specs=ins,
        out_specs=[VMEM] * len(outs),
        scratch_shapes=scratch,
        compiler_params=pltpu.CompilerParams(vmem_limit_bytes=VMEM_LIMIT),
        cost_estimate=pl.CostEstimate(flops=flops, bytes_accessed=moved, transcendentals=0),
    )


def project_kernel(momentum, gradient, factor, flipped, given, kept, total, stacked):
    step, steps = pl.program_id(0), pl.num_programs(0)
    rows, half = momentum.shape[0], given.shape[0]
    combined = momentum[...] + gradient[...].astype(f32)
    flipped[...] = combined.T
    for i, v in enumerate(split3(combined)):
        stacked[i * rows : (i + 1) * rows, :] = v
    parts = jnp.dot(stacked[...], factor[...], preferred_element_type=f32)
    part = (parts[2 * rows :] + parts[rows : 2 * rows]) + parts[:rows]

    @pl.when(step == 0)
    def _():
        total[...] = part

    @pl.when(step > 0)
    def _():
        total[...] += part

    @pl.when(step == steps - 1)
    def _():
        core = core_index()
        given[...] = total[pl.ds(pl.multiple_of((1 - core) * half, half), half), :]
        kept[...] = total[pl.ds(pl.multiple_of(core * half, half), half), :]


def project(momentum, gradient, factor):
    rows, cols = momentum.shape
    half = shape((rows // 2, RANK))
    block = pl.BlockSpec((rows, WIDE), lambda i: (0, i))
    whole = pl.BlockSpec(half.shape, lambda i: (0, 0))
    return pl.pallas_call(
        project_kernel,
        grid=(cols // WIDE,),
        out_shape=[shape((cols, rows)), half, half],
        in_specs=[block, block, pl.BlockSpec((WIDE, RANK), lambda i: (i, 0))],
        out_specs=[pl.BlockSpec((WIDE, rows), lambda i: (i, 0)), whole, whole],
        scratch_shapes=[pltpu.VMEM((rows, RANK), f32), pltpu.VMEM((3 * rows, WIDE), bf16)],
        compiler_params=pltpu.CompilerParams(vmem_limit_bytes=VMEM_ALL),
        cost_estimate=pl.CostEstimate(flops=6 * rows * cols * RANK, bytes_accessed=10 * rows * cols, transcendentals=0),
    )(momentum, gradient, factor)


def gram_kernel(*refs):
    parts, (given, kept, stacked, packed) = refs[:NY], refs[NY:]
    half, few = parts[0].shape[0], given.shape[0]
    for k in range(NY):
        stacked[k * half : (k + 1) * half, :] = parts[k][...]
    n = 0
    for i in range(BLOCKS):
        strip = dot_0(stacked[:, i * BLOCK : (i + 1) * BLOCK], stacked[:, i * BLOCK :])
        for j in range(BLOCKS - i):
            packed[n * BLOCK : (n + 1) * BLOCK, :] = strip[:, j * BLOCK : (j + 1) * BLOCK]
            n += 1
    core = core_index()
    given[...] = packed[pl.ds(pl.multiple_of((1 - core) * few, few), few), :]
    kept[...] = packed[pl.ds(pl.multiple_of(core * few, few), few), :]


def gram_halves(parts):
    few = len(UPPER) * BLOCK // 2
    half = parts[0].shape[0]
    return call(
        gram_kernel,
        [shape((few, BLOCK))] * 2 + [shape((NY * half, RANK))],
        [VMEM] * NY,
        [pltpu.VMEM((2 * few, BLOCK), f32)],
        12 * NY * half * RANK * RANK,
        4 * NY * half * RANK + 8 * few * BLOCK,
    )(*parts)


def share_kernel(swapped, out):
    rows = swapped.shape[0] // NZ
    terms = [swapped[k * rows : (k + 1) * rows, :] for k in range(NZ)]
    total = ((terms[0] + terms[1]) + (terms[2] + terms[3])) + ((terms[4] + terms[5]) + (terms[6] + terms[7]))
    for k in range(NZ):
        out[k * rows : (k + 1) * rows, :] = total


def share(swapped):
    return call(share_kernel, [shape(swapped.shape)], [VMEM], [], 0, 8 * swapped.size)(swapped)[0]


def right_kernel(mine, other, blocks, kept, given_a, given_b, projected, rows_all, cols_all, result):
    half = mine.shape[0] // NY
    eighth = result.shape[1]
    quarter = NZ * eighth
    core, odd = core_index(), lax.rem(z_index(), 2)
    for k in range(NY):
        low = pl.multiple_of(2 * k * half + core * half, half)
        high = pl.multiple_of(2 * k * half + (1 - core) * half, half)
        rows_all[pl.ds(low, half), :] = mine[k * half : (k + 1) * half, :]
        rows_all[pl.ds(high, half), :] = other[k * half : (k + 1) * half, :]
        row = pl.multiple_of(lax.rem(y_index() + k, NY) * quarter, 8)
        cols_all[:, 2 * k * half : 2 * (k + 1) * half] = blocks[pl.ds(row, quarter), :]
    projected[...] = rows_all[: 2 * half, :]
    total = jnp.dot(cols_all[...], rows_all[...], precision=precise, preferred_element_type=f32)
    for s in range(NZ):
        result[s] = total[s * eighth : (s + 1) * eighth, :]
    for s in range(NZ // 2):
        kept[s] = result[2 * s + odd]
        given_a[s] = result[2 * s + 1 - odd, :, : RANK // 2]
        given_b[s] = result[2 * s + 1 - odd, :, RANK // 2 :]


def right_sums(mine, other, blocks):
    cols, rows = blocks.shape
    quarter = cols // NY
    eighth = quarter // NZ
    return call(
        right_kernel,
        [shape((NZ // 2, eighth, RANK))] + [shape((NZ // 2, eighth, RANK // 2))] * 2 + [shape((rows, RANK))],
        [VMEM] * 3,
        [pltpu.VMEM((NY * rows, RANK), f32), pltpu.VMEM((quarter, NY * rows), f32), pltpu.VMEM((NZ, eighth, RANK), f32)],
        12 * quarter * NY * rows * RANK,
        4 * (quarter * NY * rows + NY * rows * RANK + quarter * RANK),
    )(mine, other, blocks)


def shift_kernel(kept, from_a, from_b, *outs):
    for k in range(NZ // 2):
        s = lax.rem(z_index() + 2 * k, NZ) // 2
        outs[k][:, : RANK // 2] = kept[s, :, : RANK // 2] + from_a[s]
        outs[k][:, RANK // 2 :] = kept[s, :, RANK // 2 :] + from_b[s]


def shifted(kept, from_a, from_b):
    eighth = kept.shape[1]
    return call(
        shift_kernel, [shape((eighth, RANK))] * (NZ // 2), [VMEM] * 3, [], 0, 8 * kept.size
    )(kept, from_a, from_b)


def spread_kernel(a, b, c, d, out):
    total = (a[...] + c[...]) + (b[...] + d[...])
    rows = total.shape[0]
    for k in range(NZ):
        out[k * rows : (k + 1) * rows, :] = total


def spread_sum(parts):
    rows, cols = parts[0].shape
    return call(spread_kernel, [shape((NZ * rows, cols))], [VMEM] * len(parts), [], 0, 8 * NZ * rows * cols)(*parts)[0]


def level(squares, count):
    return jnp.sqrt(jnp.maximum(squares / count, 1e-30))


def normal_kernel(right0, inverse, sent, squares):
    right = dot_t(right0[...], inverse[...])
    sums = jnp.sum(right * right, axis=0, keepdims=True)
    squares[...] = sums
    sent[...] = right / level(sums, right.shape[0])


def normalised(right0, inverse):
    quarter = right0.shape[0]
    return call(
        normal_kernel,
        [shape((quarter, RANK)), shape((1, RANK))],
        [VMEM, VMEM],
        [],
        12 * quarter * RANK * RANK,
        8 * quarter * RANK,
    )(right0, inverse)


def update_kernel(momentum, gradient, weight, basis, scale, *refs):
    parts, squares = refs[:NY], refs[NY : 2 * NY]
    new_momentum, new_factor, new_weight, factor, spread = refs[2 * NY :]
    rows, wide = momentum.shape
    step = pl.program_id(0)
    quarter = parts[0].shape[0]

    @pl.when(step == 0)
    def _():
        s = scale[...]
        for k in range(NY):
            row = pl.multiple_of(lax.rem(y_index() + k, NY) * quarter, 64)
            factor[pl.ds(row, quarter), :] = (parts[k][...] * (level(squares[k][:1], quarter) / s)).astype(bf16)
        b = basis[...]
        for i, v in enumerate((b * s, b)):
            hi = v.astype(bf16)
            spread[2 * i * rows : (2 * i + 1) * rows, :] = hi
            spread[(2 * i + 1) * rows : (2 * i + 2) * rows, :] = (v - hi.astype(f32)).astype(bf16)

    f = factor[pl.ds(pl.multiple_of(step * wide, wide), wide), :]
    new_factor[...] = f
    products = lax.dot_general(spread[...], f, (((1,), (1,)), ((), ())), preferred_element_type=f32)

    def times(i):
        return products[2 * i * rows : (2 * i + 1) * rows] + products[(2 * i + 1) * rows : (2 * i + 2) * rows]

    combined = momentum[...] + gradient[...].astype(f32)
    new_momentum[...] = combined - (1.0 - decay_rate) * times(0)
    step_size = learn_rate * (D / RANK) ** 0.5
    new_weight[...] = (weight[...].astype(f32) - step_size * times(1)).astype(bf16)


def update(momentum, gradient, weight, basis, scale, parts, squares):
    rows, cols = momentum.shape
    block = pl.BlockSpec((rows, WIDE), lambda i: (0, i))
    whole = lambda a: pl.BlockSpec(a.shape, lambda i: (0, 0))
    return pl.pallas_call(
        update_kernel,
        grid=(cols // WIDE,),
        out_shape=[shape((rows, cols)), shape((cols, RANK), bf16), shape((rows, cols), bf16)],
        in_specs=[block, block, block, whole(basis), whole(scale)] + [whole(a) for a in parts + squares],
        out_specs=[block, pl.BlockSpec((WIDE, RANK), lambda i: (i, 0)), block],
        scratch_shapes=[pltpu.VMEM((cols, RANK), bf16), pltpu.VMEM((4 * rows, RANK), bf16)],
        compiler_params=pltpu.CompilerParams(vmem_limit_bytes=40 * 1024 * 1024),
        cost_estimate=pl.CostEstimate(flops=8 * rows * cols * RANK, bytes_accessed=16 * rows * cols, transcendentals=0),
    )(momentum, gradient, weight, basis, scale, *parts, *squares)


def over_z(a):
    return lax.all_to_all(a, "dp", 0, 0, axis_index_groups=Z_GROUPS, tiled=True)


def shards(momentum, gradient, factor, weight):
    rows, cols = momentum.shape

    flipped, given, kept = project(momentum, gradient, factor)
    blocks = lax.all_to_all(flipped, "dp", 0, 0, axis_index_groups=Y_GROUPS, tiled=True)
    pair = kept + lax.ppermute(given, "tensor", OTHER_CORE)
    xs = [pair] + [lax.ppermute(pair, "tensor", from_x(k)) for k in range(1, NX)]
    mine = (xs[0] + xs[2]) + (xs[1] + xs[3])
    mine = [mine] + [lax.ppermute(mine, "dp", from_y(k)) for k in range(1, NY)]
    mine, blocks = lax.optimization_barrier((mine, blocks))

    gram_given, gram_kept, stacked = gram_halves(mine)
    gram_pair = gram_kept + lax.ppermute(gram_given, "tensor", OTHER_CORE)
    other = lax.ppermute(stacked, "tensor", OTHER_CORE)

    right_kept, right_a, right_b, projected = right_sums(stacked, other, blocks)
    right_a = lax.ppermute(right_a, "dp", to_neighbour(0))
    right_b = lax.ppermute(right_b, "dp", to_neighbour(1))
    gram_shares = share(over_z(gram_pair))
    gram_shares, right_a, right_b = lax.optimization_barrier((gram_shares, right_a, right_b))
    pairs = shifted(right_kept, right_a, right_b)
    pairs = [pairs[0]] + [lax.ppermute(pairs[k], "dp", from_z(NZ - 2 * k)) for k in range(1, NZ // 2)]
    gram_half = over_z(gram_shares)
    gram_other = lax.ppermute(gram_half, "tensor", OTHER_CORE)
    right0 = spread_sum(pairs)
    inverse = inverse_cholesky(gram_half, gram_other, right0)
    right0 = over_z(right0)

    basis = dot_t(projected, inverse)
    basis, right0 = lax.optimization_barrier((basis, right0))
    sent, squares = normalised(right0, inverse)
    sent = sent.astype(jnp.float16)
    sent_y = [sent] + [lax.ppermute(sent, "dp", from_y(k)) for k in range(1, NY)]
    squares_x = [squares] + [lax.ppermute(squares, "tensor", from_x(k)) for k in range(1, NX)]
    total = (squares_x[0] + squares_x[2]) + (squares_x[1] + squares_x[3])
    total = total + lax.ppermute(total, "tensor", OTHER_CORE)
    both = jnp.concatenate([squares, total], 0)
    both_y = [both] + [lax.ppermute(both, "dp", from_y(k)) for k in range(1, NY)]
    both_y, sent_y = lax.optimization_barrier((both_y, sent_y))
    total = (both_y[0][1:] + both_y[2][1:]) + (both_y[1][1:] + both_y[3][1:])
    scale = jnp.sqrt(total / (cols * 2 * NX) + epsilon)
    sent_y = [a.astype(f32) for a in sent_y]
    return update(momentum, gradient, weight, basis, scale, sent_y, both_y)


def solution(mesh):
    in_specs = (P("dp", "tensor"), P("dp", "tensor"), P("tensor", None), P("dp", "tensor"))
    out_specs = (P("dp", "tensor"), P("tensor", None), P("dp", "tensor"))
    return jax.shard_map(shards, mesh=mesh, in_specs=in_specs, out_specs=out_specs, check_vma=False)
```

profile of v0, /device:TPU:4, one launch (start us, length us, event | category | flops | bytes accessed | tf_op | source)
XLA Modules:
  0.0 171.0 jit_solution(14650642193199969596)
XLA Ops:
  0.6 4.8 %shard_map.67 = (f32[1792,256]{1,0:T(8,128)}, f32[128,512]{1,0:T(8,128)}, f32[128,512]{1,0:T(8,128)}) custom-call(f32[256,1792]{1,0:T(8,128)} %momentum.3, bf16[256,1792]{1,0:T(8,128)(2,1)} %gradient.3, bf16[1792,512]{1,0:T(8,128)(2,1)} %factor.1), custom_call_target="tpu_custom_call" | custom-call | flops 1409286144 | bytes 4587520 | tf_op jit(solution)/shard_map/pallas_call | solution.py:226
  5.5 4.6 %all-to-all-start = ((f32[4,448,256]{2,1,0:T(8,128)}), f32[4,448,256]{2,1,0:T(8,128)S(1)}, u32[]{:S(2)}, u32[]{:S(2)}) async-start(f32[4,448,256]{2,1,0:T(8,128)} %bitcast.15), calls=%async_computation | async-start | bytes 3670016 | tf_op jit(solution)/shard_map/all_to_all | solution.py:420
  10.1 1.5 collective-permute-done
  11.7 1.3 collective-permute-start.3
  13.8 2.7 %collective-permute-start.1 = (f32[128,512]{1,0:T(8,128)S(1)}, f32[128,512]{1,0:T(8,128)S(1)}, u32[]{:S(2)}, u32[]{:S(2)}) collective-permute-start(f32[128,512]{1,0:T(8,128)S(1)} %add.42), channel_id=1, source_target_pairs={{4,0},{5,1},{6,2},{7,3},{0,4},{1,5},{2,6},{3,7},{12,8},{13,9},{14,... | collective-permute-start | bytes 786440 | tf_op jit(solution)/shard_map/ppermute | solution.py:422
  16.4 4.5 %collective-permute-done.3 = f32[128,512]{1,0:T(8,128)S(1)} collective-permute-done((f32[128,512]{1,0:T(8,128)S(1)}, f32[128,512]{1,0:T(8,128)S(1)}, u32[]{:S(2)}, u32[]{:S(2)}) %collective-permute-start.3) | collective-permute-done | bytes 262176 | tf_op jit(solution)/shard_map/ppermute | solution.py:422
  20.9 1.2 collective-permute-done.2
  22.1 3.6 %collective-permute-done.1 = f32[128,512]{1,0:T(8,128)S(1)} collective-permute-done((f32[128,512]{1,0:T(8,128)S(1)}, f32[128,512]{1,0:T(8,128)S(1)}, u32[]{:S(2)}, u32[]{:S(2)}) %collective-permute-start.1) | collective-permute-done | bytes 262176 | tf_op jit(solution)/shard_map/ppermute | solution.py:422
  25.8 2.1 %collective-permute-start.6 = (f32[128,512]{1,0:T(8,128)S(1)}, f32[128,512]{1,0:T(8,128)S(1)}, u32[]{:S(2)}, u32[]{:S(2)}) collective-permute-start(f32[128,512]{1,0:T(8,128)S(1)} %add_add_fusion.refs_0_), channel_id=1, source_target_pairs={{192,0},{200,8},{208,16},{216,24},{224,32},{232,40},{240,48},{248,... | collective-permute-start | bytes 786440 | tf_op jit(solution)/shard_map/ppermute | solution.py:424
  27.9 2.7 %collective-permute-start.5 = (f32[128,512]{1,0:T(8,128)S(1)}, f32[128,512]{1,0:T(8,128)S(1)}, u32[]{:S(2)}, u32[]{:S(2)}) collective-permute-start(f32[128,512]{1,0:T(8,128)S(1)} %add_add_fusion.refs_0_), channel_id=1, source_target_pairs={{128,0},{136,8},{144,16},{152,24},{160,32},{168,40},{176,48},{184,... | collective-permute-start | bytes 786440 | tf_op jit(solution)/shard_map/ppermute | solution.py:424
  30.6 1.5 collective-permute-start.4
  32.0 8.6 %collective-permute-done.6.refs_3_ = f32[128,512]{1,0:T(8,128)S(1)} collective-permute-done((f32[128,512]{1,0:T(8,128)S(1)}, f32[128,512]{1,0:T(8,128)S(1)}, u32[]{:S(2)}, u32[]{:S(2)}) %collective-permute-start.6) | collective-permute-done | bytes 262176 | tf_op jit(solution)/shard_map/ppermute | solution.py:424
  40.6 4.2 %collective-permute-done.5.refs_2_ = f32[128,512]{1,0:T(8,128)S(1)} collective-permute-done((f32[128,512]{1,0:T(8,128)S(1)}, f32[128,512]{1,0:T(8,128)S(1)}, u32[]{:S(2)}, u32[]{:S(2)}) %collective-permute-start.5) | collective-permute-done | bytes 262176 | tf_op jit(solution)/shard_map/ppermute | solution.py:424
  46.3 0.9 copy-done.6
  48.2 1.7 %shard_map.68 = (f32[640,128]{1,0:T(8,128)S(1)}, f32[640,128]{1,0:T(8,128)S(1)}, f32[512,512]{1,0:T(8,128)S(1)}) custom-call(f32[128,512]{1,0:T(8,128)S(1)} %add_add_fusion.refs_0_, f32[128,512]{1,0:T(8,128)S(1)} %copy-done.8, f32[128,512]{1,0:T(8,128)S(1)} %copy-done.6, f32[128,512]{1,0:T(8,128)S(1)} %collective-permute-done.6.refs_3_), custom_call_target="tpu_custom_call" | custom-call | flops 1610612736 | bytes 1703936 | tf_op jit(solution)/shard_map/pallas_call | solution.py:257
  50.6 2.6 %collective-permute-done.8 = f32[640,128]{1,0:T(8,128)S(1)} collective-permute-done((f32[640,128]{1,0:T(8,128)S(1)}, f32[640,128]{1,0:T(8,128)S(1)}, u32[]{:S(2)}, u32[]{:S(2)}) %collective-permute-start.8) | collective-permute-done | bytes 327712 | tf_op jit(solution)/shard_map/ppermute | solution.py:428
  53.9 8.5 %all-to-all-start.1 = ((f32[8,80,128]{2,1,0:T(8,128)}), f32[8,80,128]{2,1,0:T(8,128)S(1)}, u32[]{:S(2)}, u32[]{:S(2)}) async-start(f32[8,80,128]{2,1,0:T(8,128)} %bitcast.2), calls=%async_computation.1 | async-start | bytes 655360 | tf_op jit(solution)/shard_map/all_to_all | solution.py:413
  62.4 1.2 copy-done.4
  63.6 5.4 %shard_map.69 = (f32[4,56,512]{2,1,0:T(8,128)S(1)}, f32[4,56,256]{2,1,0:T(8,128)}, f32[4,56,256]{2,1,0:T(8,128)}, f32[256,512]{1,0:T(8,128)S(1)}) custom-call(f32[512,512]{1,0:T(8,128)S(1)} %copy-done.4, f32[512,512]{1,0:T(8,128)} %collective-permute-done.7.other, f32[1792,256]{1,0:T(8,128)S(1)} %bitcast.10), custom_call_target="tpu_custom_call" | custom-call | flops 2818572288 | bytes 4849664 | tf_op jit(solution)/shard_map/pallas_call | solution.py:305
  69.0 2.0 %collective-permute-start.9 = (f32[4,56,256]{2,1,0:T(8,128)}, f32[4,56,256]{2,1,0:T(8,128)S(1)}, u32[]{:S(2)}, u32[]{:S(2)}) collective-permute-start(f32[4,56,256]{2,1,0:T(8,128)} %get-tuple-element.49), channel_id=1, source_target_pairs={{0,8},{8,0},{16,24},{24,16},{32,40},{40,32},{48,56},{56,48},{64,72... | collective-permute-start | bytes 688136 | tf_op jit(solution)/shard_map/ppermute | solution.py:432
  71.0 2.7 %collective-permute-start.10 = (f32[4,56,256]{2,1,0:T(8,128)}, f32[4,56,256]{2,1,0:T(8,128)S(1)}, u32[]{:S(2)}, u32[]{:S(2)}) collective-permute-start(f32[4,56,256]{2,1,0:T(8,128)} %get-tuple-element.50), channel_id=1, source_target_pairs={{0,56},{8,16},{16,8},{24,32},{32,24},{40,48},{48,40},{56,0},{64,12... | collective-permute-start | bytes 688136 | tf_op jit(solution)/shard_map/ppermute | solution.py:433
  73.7 2.3 %all-to-all-done.1 = f32[8,80,128]{2,1,0:T(8,128)S(1)} async-done(((f32[8,80,128]{2,1,0:T(8,128)}), f32[8,80,128]{2,1,0:T(8,128)S(1)}, u32[]{:S(2)}, u32[]{:S(2)}) %all-to-all-start.1) | async-done | bytes 327712 | tf_op jit(solution)/shard_map/all_to_all | solution.py:413
  77.0 3.0 %collective-permute-done.10.from_b = f32[4,56,256]{2,1,0:T(8,128)S(1)} collective-permute-done((f32[4,56,256]{2,1,0:T(8,128)}, f32[4,56,256]{2,1,0:T(8,128)S(1)}, u32[]{:S(2)}, u32[]{:S(2)}) %collective-permute-start.10) | collective-permute-done | bytes 229408 | tf_op jit(solution)/shard_map/ppermute | solution.py:433
  79.9 5.1 %all-to-all-start.2 = ((f32[8,80,128]{2,1,0:T(8,128)}), f32[8,80,128]{2,1,0:T(8,128)S(1)}, u32[]{:S(2)}, u32[]{:S(2)}) async-start(f32[8,80,128]{2,1,0:T(8,128)} %bitcast.4), calls=%async_computation.2 | async-start | bytes 655360 | tf_op jit(solution)/shard_map/all_to_all | solution.py:413
  85.1 3.0 %collective-permute-start.12 = (f32[56,512]{1,0:T(8,128)S(1)}, f32[56,512]{1,0:T(8,128)S(1)}, u32[]{:S(2)}, u32[]{:S(2)}) collective-permute-start(f32[56,512]{1,0:T(8,128)S(1)} %get-tuple-element.56), channel_id=1, source_target_pairs={{48,0},{56,8},{0,16},{8,24},{16,32},{24,40},{32,48},{40,56},{112,6... | collective-permute-start | bytes 344072 | tf_op jit(solution)/shard_map/ppermute | solution.py:437
  88.1 3.6 %collective-permute-start.13 = (f32[56,512]{1,0:T(8,128)S(1)}, f32[56,512]{1,0:T(8,128)S(1)}, u32[]{:S(2)}, u32[]{:S(2)}) collective-permute-start(f32[56,512]{1,0:T(8,128)S(1)} %get-tuple-element.57), channel_id=1, source_target_pairs={{32,0},{40,8},{48,16},{56,24},{0,32},{8,40},{16,48},{24,56},{96,64... | collective-permute-start | bytes 344072 | tf_op jit(solution)/shard_map/ppermute | solution.py:437
  91.7 3.6 %collective-permute-start.14 = (f32[56,512]{1,0:T(8,128)S(1)}, f32[56,512]{1,0:T(8,128)S(1)}, u32[]{:S(2)}, u32[]{:S(2)}) collective-permute-start(f32[56,512]{1,0:T(8,128)S(1)} %get-tuple-element.58), channel_id=1, source_target_pairs={{16,0},{24,8},{32,16},{40,24},{48,32},{56,40},{0,48},{8,56},{80,64... | collective-permute-start | bytes 344072 | tf_op jit(solution)/shard_map/ppermute | solution.py:437
  95.2 4.4 %all-to-all-done.2 = f32[8,80,128]{2,1,0:T(8,128)S(1)} async-done(((f32[8,80,128]{2,1,0:T(8,128)}), f32[8,80,128]{2,1,0:T(8,128)S(1)}, u32[]{:S(2)}, u32[]{:S(2)}) %all-to-all-start.2) | async-done | bytes 327712 | tf_op jit(solution)/shard_map/all_to_all | solution.py:413
  99.6 2.4 %collective-permute-done.12.b = f32[56,512]{1,0:T(8,128)S(1)} collective-permute-done((f32[56,512]{1,0:T(8,128)S(1)}, f32[56,512]{1,0:T(8,128)S(1)}, u32[]{:S(2)}, u32[]{:S(2)}) %collective-permute-start.12) | collective-permute-done | bytes 114720 | tf_op jit(solution)/shard_map/ppermute | solution.py:437
  102.0 3.2 %collective-permute-done.13.c = f32[56,512]{1,0:T(8,128)S(1)} collective-permute-done((f32[56,512]{1,0:T(8,128)S(1)}, f32[56,512]{1,0:T(8,128)S(1)}, u32[]{:S(2)}, u32[]{:S(2)}) %collective-permute-start.13) | collective-permute-done | bytes 114720 | tf_op jit(solution)/shard_map/ppermute | solution.py:437
  105.2 1.0 shard_map.72.after
  106.2 3.8 %all-to-all-start.3 = ((f32[8,56,512]{2,1,0:T(8,128)}), f32[8,56,512]{2,1,0:T(8,128)S(1)}, u32[]{:S(2)}, u32[]{:S(2)}) async-start(f32[8,56,512]{2,1,0:T(8,128)} %bitcast.6), calls=%async_computation.3 | async-start | bytes 1835008 | tf_op jit(solution)/shard_map/all_to_all | solution.py:413
  110.0 21.0 %shard_map.73.inverse = f32[512,512]{1,0:T(8,128)S(1)} custom-call(f32[640,128]{1,0:T(8,128)S(1)} %bitcast.14, f32[640,128]{1,0:T(8,128)S(1)} %collective-permute-done.11.other_ref, f32[448,512]{1,0:T(8,128)} %shard_map.72.after), custom_call_target="tpu_custom_call" | custom-call | flops 10737418240 | bytes 2097152 | tf_op jit(solution)/shard_map/pallas_call | solution.py:132
  131.0 1.1 fusion.basis
  132.1 3.3 %all-to-all-done.3 = f32[8,56,512]{2,1,0:T(8,128)S(1)} async-done(((f32[8,56,512]{2,1,0:T(8,128)}), f32[8,56,512]{2,1,0:T(8,128)S(1)}, u32[]{:S(2)}, u32[]{:S(2)}) %all-to-all-start.3) | async-done | bytes 917536 | tf_op jit(solution)/shard_map/all_to_all | solution.py:413
  135.3 1.8 %shard_map.74 = (f32[448,512]{1,0:T(8,128)S(1)}, f32[1,512]{1,0:T(1,128)S(1)}) custom-call(f32[448,512]{1,0:T(8,128)S(1)} %bitcast.12, f32[512,512]{1,0:T(8,128)S(1)} %shard_map.73.inverse), custom_call_target="tpu_custom_call" | custom-call | flops 1409286144 | bytes 1835008 | tf_op jit(solution)/shard_map/pallas_call | solution.py:354
  137.3 1.9 %collective-permute-start.23 = (f16[448,512]{1,0:T(8,128)(2,1)S(1)}, f16[448,512]{1,0:T(8,128)(2,1)S(1)}, u32[]{:S(2)}, u32[]{:S(2)}) collective-permute-start(f16[448,512]{1,0:T(8,128)(2,1)S(1)} %convert_element_type.15), channel_id=1, source_target_pairs={{128,0},{136,8},{144,16},{152,24},{160,32},{168,40},{176,48},{184,... | collective-permute-start | bytes 1376264 | tf_op jit(solution)/shard_map/ppermute | solution.py:448
  139.2 1.4 collective-permute-start.22
  140.5 1.2 collective-permute-start.17
  142.6 1.6 collective-permute-done.17
  144.1 2.1 %collective-permute-start.15 = (f32[1,512]{1,0:T(1,128)S(1)}, f32[1,512]{1,0:T(1,128)S(1)}, u32[]{:S(2)}, u32[]{:S(2)}) collective-permute-start(f32[1,512]{1,0:T(1,128)S(1)} %get-tuple-element.61), channel_id=1, source_target_pairs={{4,0},{5,1},{6,2},{7,3},{0,4},{1,5},{2,6},{3,7},{12,8},{13,9},{14,... | collective-permute-start | bytes 6152 | tf_op jit(solution)/shard_map/ppermute | solution.py:449
  146.2 3.0 %collective-permute-done.15 = f32[1,512]{1,0:T(1,128)S(1)} collective-permute-done((f32[1,512]{1,0:T(1,128)S(1)}, f32[1,512]{1,0:T(1,128)S(1)}, u32[]{:S(2)}, u32[]{:S(2)}) %collective-permute-start.15) | collective-permute-done | bytes 2080 | tf_op jit(solution)/shard_map/ppermute | solution.py:449
  149.3 1.1 collective-permute-done.18
  151.4 2.2 %collective-permute-start.20 = (f32[2,512]{1,0:T(2,128)S(1)}, f32[2,512]{1,0:T(2,128)S(1)}, u32[]{:S(2)}, u32[]{:S(2)}) collective-permute-start(f32[2,512]{1,0:T(2,128)S(1)} %pad_maximum_fusion.refs_4_), channel_id=1, source_target_pairs={{128,0},{136,8},{144,16},{152,24},{160,32},{168,40},{176,48},{184,... | collective-permute-start | bytes 12296 | tf_op jit(solution)/shard_map/ppermute | solution.py:453
  153.6 7.4 %collective-permute-done.21.refs_7_ = f32[2,512]{1,0:T(2,128)S(1)} collective-permute-done((f32[2,512]{1,0:T(2,128)S(1)}, f32[2,512]{1,0:T(2,128)S(1)}, u32[]{:S(2)}, u32[]{:S(2)}) %collective-permute-start.21) | collective-permute-done | bytes 4128 | tf_op jit(solution)/shard_map/ppermute | solution.py:453
  161.0 3.6 %collective-permute-done.19.refs_5_ = f32[2,512]{1,0:T(2,128)S(1)} collective-permute-done((f32[2,512]{1,0:T(2,128)S(1)}, f32[2,512]{1,0:T(2,128)S(1)}, u32[]{:S(2)}, u32[]{:S(2)}) %collective-permute-start.19) | collective-permute-done | bytes 4128 | tf_op jit(solution)/shard_map/ppermute | solution.py:453
  165.1 1.1 copy-done
  166.7 4.3 %shard_map.75 = (f32[256,1792]{1,0:T(8,128)}, bf16[1792,512]{1,0:T(8,128)(2,1)}, bf16[256,1792]{1,0:T(8,128)(2,1)}) custom-call(f32[256,1792]{1,0:T(8,128)S(1)} %copy-done, bf16[256,1792]{1,0:T(8,128)(2,1)S(1)} %copy-done.1, bf16[256,1792]{1,0:T(8,128)(2,1)S(1)} %copy-done.2, f32[256,512]{1,0:T(8,128)S(1)} %fusion.basis, f32[1,512]{1,0:T(1,128)S(1)} %add_sqrt_fusion.scale, ...), custom_call_target="tpu_custom_call" | custom-call | flops 1879048192 | bytes 7340032 | tf_op jit(solution)/shard_map/pallas_call | solution.py:400
  (54 shorter events, 8.8 us)
Async XLA Ops:
  5.5 4.6 %copy-start.10 = (f32[128,512]{1,0:T(8,128)S(1)}, f32[128,512]{1,0:T(8,128)}, u32[]{:S(2)}) copy-start(f32[128,512]{1,0:T(8,128)} %get-tuple-element.38) | copy-start | bytes 786436
  5.5 6.2 %copy-start.9 = (f32[128,512]{1,0:T(8,128)S(1)}, f32[128,512]{1,0:T(8,128)}, u32[]{:S(2)}) copy-start(f32[128,512]{1,0:T(8,128)} %get-tuple-element.37) | copy-start | bytes 786436
  5.5 40.8 %all-to-all-start = ((f32[4,448,256]{2,1,0:T(8,128)}), f32[4,448,256]{2,1,0:T(8,128)S(1)}, u32[]{:S(2)}, u32[]{:S(2)}) async-start(f32[4,448,256]{2,1,0:T(8,128)} %bitcast.15), calls=%async_computation | async-start | bytes 3670016 | tf_op jit(solution)/shard_map/all_to_all | solution.py:420
  10.1 1.5 collective-permute-start
  11.7 9.2 %collective-permute-start.3 = (f32[128,512]{1,0:T(8,128)S(1)}, f32[128,512]{1,0:T(8,128)S(1)}, u32[]{:S(2)}, u32[]{:S(2)}) collective-permute-start(f32[128,512]{1,0:T(8,128)S(1)} %add.42), channel_id=1, source_target_pairs={{6,0},{7,1},{0,2},{1,3},{2,4},{3,5},{4,6},{5,7},{14,8},{15,9},{8,1... | collective-permute-start | bytes 786440 | tf_op jit(solution)/shard_map/ppermute | solution.py:422
  12.9 9.2 %collective-permute-start.2 = (f32[128,512]{1,0:T(8,128)S(1)}, f32[128,512]{1,0:T(8,128)S(1)}, u32[]{:S(2)}, u32[]{:S(2)}) collective-permute-start(f32[128,512]{1,0:T(8,128)S(1)} %add.42), channel_id=1, source_target_pairs={{2,0},{3,1},{4,2},{5,3},{6,4},{7,5},{0,6},{1,7},{10,8},{11,9},{12,... | collective-permute-start | bytes 786440 | tf_op jit(solution)/shard_map/ppermute | solution.py:422
  13.8 11.9 %collective-permute-start.1 = (f32[128,512]{1,0:T(8,128)S(1)}, f32[128,512]{1,0:T(8,128)S(1)}, u32[]{:S(2)}, u32[]{:S(2)}) collective-permute-start(f32[128,512]{1,0:T(8,128)S(1)} %add.42), channel_id=1, source_target_pairs={{4,0},{5,1},{6,2},{7,3},{0,4},{1,5},{2,6},{3,7},{12,8},{13,9},{14,... | collective-permute-start | bytes 786440 | tf_op jit(solution)/shard_map/ppermute | solution.py:422
  25.8 14.8 %collective-permute-start.6 = (f32[128,512]{1,0:T(8,128)S(1)}, f32[128,512]{1,0:T(8,128)S(1)}, u32[]{:S(2)}, u32[]{:S(2)}) collective-permute-start(f32[128,512]{1,0:T(8,128)S(1)} %add_add_fusion.refs_0_), channel_id=1, source_target_pairs={{192,0},{200,8},{208,16},{216,24},{224,32},{232,40},{240,48},{248,... | collective-permute-start | bytes 786440 | tf_op jit(solution)/shard_map/ppermute | solution.py:424
  27.9 17.0 %collective-permute-start.5 = (f32[128,512]{1,0:T(8,128)S(1)}, f32[128,512]{1,0:T(8,128)S(1)}, u32[]{:S(2)}, u32[]{:S(2)}) collective-permute-start(f32[128,512]{1,0:T(8,128)S(1)} %add_add_fusion.refs_0_), channel_id=1, source_target_pairs={{128,0},{136,8},{144,16},{152,24},{160,32},{168,40},{176,48},{184,... | collective-permute-start | bytes 786440 | tf_op jit(solution)/shard_map/ppermute | solution.py:424
  30.6 15.0 %collective-permute-start.4 = (f32[128,512]{1,0:T(8,128)S(1)}, f32[128,512]{1,0:T(8,128)S(1)}, u32[]{:S(2)}, u32[]{:S(2)}) collective-permute-start(f32[128,512]{1,0:T(8,128)S(1)} %add_add_fusion.refs_0_), channel_id=1, source_target_pairs={{64,0},{72,8},{80,16},{88,24},{96,32},{104,40},{112,48},{120,56},{... | collective-permute-start | bytes 786440 | tf_op jit(solution)/shard_map/ppermute | solution.py:424
  44.9 0.7 copy-start.5
  45.6 0.7 copy-start.7
  46.3 1.0 copy-start.6
  47.2 0.9 copy-start.8
  49.9 12.4 %copy-start.3 = (f32[512,512]{1,0:T(8,128)}, f32[512,512]{1,0:T(8,128)S(1)}, u32[]{:S(2)}) copy-start(f32[512,512]{1,0:T(8,128)S(1)} %get-tuple-element.44.mine) | copy-start | bytes 3145732
  50.0 12.4 %collective-permute-start.7 = (f32[512,512]{1,0:T(8,128)S(1)}, f32[512,512]{1,0:T(8,128)}, u32[]{:S(2)}, u32[]{:S(2)}) collective-permute-start(f32[512,512]{1,0:T(8,128)S(1)} %get-tuple-element.44.mine), channel_id=1, source_target_pairs={{1,0},{0,1},{3,2},{2,3},{5,4},{4,5},{7,6},{6,7},{9,8},{8,9},{11,10... | collective-permute-start | bytes 3145736 | tf_op jit(solution)/shard_map/ppermute | solution.py:429
  50.1 3.1 %collective-permute-start.8 = (f32[640,128]{1,0:T(8,128)S(1)}, f32[640,128]{1,0:T(8,128)S(1)}, u32[]{:S(2)}, u32[]{:S(2)}) collective-permute-start(f32[640,128]{1,0:T(8,128)S(1)} %get-tuple-element.48), channel_id=1, source_target_pairs={{1,0},{0,1},{3,2},{2,3},{5,4},{4,5},{7,6},{6,7},{9,8},{8,9},{11,10... | collective-permute-start | bytes 983048 | tf_op jit(solution)/shard_map/ppermute | solution.py:428
  53.9 22.1 %all-to-all-start.1 = ((f32[8,80,128]{2,1,0:T(8,128)}), f32[8,80,128]{2,1,0:T(8,128)S(1)}, u32[]{:S(2)}, u32[]{:S(2)}) async-start(f32[8,80,128]{2,1,0:T(8,128)} %bitcast.2), calls=%async_computation.1 | async-start | bytes 655360 | tf_op jit(solution)/shard_map/all_to_all | solution.py:413
  62.4 1.2 copy-start.4
  69.0 8.0 %collective-permute-start.9 = (f32[4,56,256]{2,1,0:T(8,128)}, f32[4,56,256]{2,1,0:T(8,128)S(1)}, u32[]{:S(2)}, u32[]{:S(2)}) collective-permute-start(f32[4,56,256]{2,1,0:T(8,128)} %get-tuple-element.49), channel_id=1, source_target_pairs={{0,8},{8,0},{16,24},{24,16},{32,40},{40,32},{48,56},{56,48},{64,72... | collective-permute-start | bytes 688136 | tf_op jit(solution)/shard_map/ppermute | solution.py:432
  71.0 8.9 %collective-permute-start.10 = (f32[4,56,256]{2,1,0:T(8,128)}, f32[4,56,256]{2,1,0:T(8,128)S(1)}, u32[]{:S(2)}, u32[]{:S(2)}) collective-permute-start(f32[4,56,256]{2,1,0:T(8,128)} %get-tuple-element.50), channel_id=1, source_target_pairs={{0,56},{8,16},{16,8},{24,32},{32,24},{40,48},{48,40},{56,0},{64,12... | collective-permute-start | bytes 688136 | tf_op jit(solution)/shard_map/ppermute | solution.py:433
  79.9 19.7 %all-to-all-start.2 = ((f32[8,80,128]{2,1,0:T(8,128)}), f32[8,80,128]{2,1,0:T(8,128)S(1)}, u32[]{:S(2)}, u32[]{:S(2)}) async-start(f32[8,80,128]{2,1,0:T(8,128)} %bitcast.4), calls=%async_computation.2 | async-start | bytes 655360 | tf_op jit(solution)/shard_map/all_to_all | solution.py:413
  85.1 16.9 %collective-permute-start.12 = (f32[56,512]{1,0:T(8,128)S(1)}, f32[56,512]{1,0:T(8,128)S(1)}, u32[]{:S(2)}, u32[]{:S(2)}) collective-permute-start(f32[56,512]{1,0:T(8,128)S(1)} %get-tuple-element.56), channel_id=1, source_target_pairs={{48,0},{56,8},{0,16},{8,24},{16,32},{24,40},{32,48},{40,56},{112,6... | collective-permute-start | bytes 344072 | tf_op jit(solution)/shard_map/ppermute | solution.py:437
  88.1 17.1 %collective-permute-start.13 = (f32[56,512]{1,0:T(8,128)S(1)}, f32[56,512]{1,0:T(8,128)S(1)}, u32[]{:S(2)}, u32[]{:S(2)}) collective-permute-start(f32[56,512]{1,0:T(8,128)S(1)} %get-tuple-element.57), channel_id=1, source_target_pairs={{32,0},{40,8},{48,16},{56,24},{0,32},{8,40},{16,48},{24,56},{96,64... | collective-permute-start | bytes 344072 | tf_op jit(solution)/shard_map/ppermute | solution.py:437
  91.7 13.5 %collective-permute-start.14 = (f32[56,512]{1,0:T(8,128)S(1)}, f32[56,512]{1,0:T(8,128)S(1)}, u32[]{:S(2)}, u32[]{:S(2)}) collective-permute-start(f32[56,512]{1,0:T(8,128)S(1)} %get-tuple-element.58), channel_id=1, source_target_pairs={{16,0},{24,8},{32,16},{40,24},{48,32},{56,40},{0,48},{8,56},{80,64... | collective-permute-start | bytes 344072 | tf_op jit(solution)/shard_map/ppermute | solution.py:437
  99.6 10.4 %collective-permute-start.11 = (f32[640,128]{1,0:T(8,128)S(1)}, f32[640,128]{1,0:T(8,128)S(1)}, u32[]{:S(2)}, u32[]{:S(2)}) collective-permute-start(f32[640,128]{1,0:T(8,128)S(1)} %bitcast.13), channel_id=1, source_target_pairs={{1,0},{0,1},{3,2},{2,3},{5,4},{4,5},{7,6},{6,7},{9,8},{8,9},{11,10... | collective-permute-start | bytes 983048 | tf_op jit(solution)/shard_map/ppermute | solution.py:439
  106.2 29.2 %all-to-all-start.3 = ((f32[8,56,512]{2,1,0:T(8,128)}), f32[8,56,512]{2,1,0:T(8,128)S(1)}, u32[]{:S(2)}, u32[]{:S(2)}) async-start(f32[8,56,512]{2,1,0:T(8,128)} %bitcast.6), calls=%async_computation.3 | async-start | bytes 1835008 | tf_op jit(solution)/shard_map/all_to_all | solution.py:413
  137.2 27.3 %collective-permute-start.24 = (f16[448,512]{1,0:T(8,128)(2,1)S(1)}, f16[448,512]{1,0:T(8,128)(2,1)S(1)}, u32[]{:S(2)}, u32[]{:S(2)}) collective-permute-start(f16[448,512]{1,0:T(8,128)(2,1)S(1)} %convert_element_type.15), channel_id=1, source_target_pairs={{192,0},{200,8},{208,16},{216,24},{224,32},{232,40},{240,48},{248,... | collective-permute-start | bytes 1376264 | tf_op jit(solution)/shard_map/ppermute | solution.py:448
  137.3 27.3 %collective-permute-start.23 = (f16[448,512]{1,0:T(8,128)(2,1)S(1)}, f16[448,512]{1,0:T(8,128)(2,1)S(1)}, u32[]{:S(2)}, u32[]{:S(2)}) collective-permute-start(f16[448,512]{1,0:T(8,128)(2,1)S(1)} %convert_element_type.15), channel_id=1, source_target_pairs={{128,0},{136,8},{144,16},{152,24},{160,32},{168,40},{176,48},{184,... | collective-permute-start | bytes 1376264 | tf_op jit(solution)/shard_map/ppermute | solution.py:448
  139.2 25.4 %collective-permute-start.22 = (f16[448,512]{1,0:T(8,128)(2,1)S(1)}, f16[448,512]{1,0:T(8,128)(2,1)S(1)}, u32[]{:S(2)}, u32[]{:S(2)}) collective-permute-start(f16[448,512]{1,0:T(8,128)(2,1)S(1)} %convert_element_type.15), channel_id=1, source_target_pairs={{64,0},{72,8},{80,16},{88,24},{96,32},{104,40},{112,48},{120,56},{... | collective-permute-start | bytes 1376264 | tf_op jit(solution)/shard_map/ppermute | solution.py:448
  140.5 3.6 %collective-permute-start.17 = (f32[1,512]{1,0:T(1,128)S(1)}, f32[1,512]{1,0:T(1,128)S(1)}, u32[]{:S(2)}, u32[]{:S(2)}) collective-permute-start(f32[1,512]{1,0:T(1,128)S(1)} %get-tuple-element.61), channel_id=1, source_target_pairs={{6,0},{7,1},{0,2},{1,3},{2,4},{3,5},{4,6},{5,7},{14,8},{15,9},{8,1... | collective-permute-start | bytes 6152 | tf_op jit(solution)/shard_map/ppermute | solution.py:449
  141.7 4.5 %collective-permute-start.16 = (f32[1,512]{1,0:T(1,128)S(1)}, f32[1,512]{1,0:T(1,128)S(1)}, u32[]{:S(2)}, u32[]{:S(2)}) collective-permute-start(f32[1,512]{1,0:T(1,128)S(1)} %get-tuple-element.61), channel_id=1, source_target_pairs={{2,0},{3,1},{4,2},{5,3},{6,4},{7,5},{0,6},{1,7},{10,8},{11,9},{12,... | collective-permute-start | bytes 6152 | tf_op jit(solution)/shard_map/ppermute | solution.py:449
  144.1 5.1 %collective-permute-start.15 = (f32[1,512]{1,0:T(1,128)S(1)}, f32[1,512]{1,0:T(1,128)S(1)}, u32[]{:S(2)}, u32[]{:S(2)}) collective-permute-start(f32[1,512]{1,0:T(1,128)S(1)} %get-tuple-element.61), channel_id=1, source_target_pairs={{4,0},{5,1},{6,2},{7,3},{0,4},{1,5},{2,6},{3,7},{12,8},{13,9},{14,... | collective-permute-start | bytes 6152 | tf_op jit(solution)/shard_map/ppermute | solution.py:449
  149.2 1.2 collective-permute-start.18
  150.5 10.5 %collective-permute-start.21 = (f32[2,512]{1,0:T(2,128)S(1)}, f32[2,512]{1,0:T(2,128)S(1)}, u32[]{:S(2)}, u32[]{:S(2)}) collective-permute-start(f32[2,512]{1,0:T(2,128)S(1)} %pad_maximum_fusion.refs_4_), channel_id=1, source_target_pairs={{192,0},{200,8},{208,16},{216,24},{224,32},{232,40},{240,48},{248,... | collective-permute-start | bytes 12296 | tf_op jit(solution)/shard_map/ppermute | solution.py:453
  151.4 9.6 %collective-permute-start.20 = (f32[2,512]{1,0:T(2,128)S(1)}, f32[2,512]{1,0:T(2,128)S(1)}, u32[]{:S(2)}, u32[]{:S(2)}) collective-permute-start(f32[2,512]{1,0:T(2,128)S(1)} %pad_maximum_fusion.refs_4_), channel_id=1, source_target_pairs={{128,0},{136,8},{144,16},{152,24},{160,32},{168,40},{176,48},{184,... | collective-permute-start | bytes 12296 | tf_op jit(solution)/shard_map/ppermute | solution.py:453
  160.9 3.6 %collective-permute-start.19 = (f32[2,512]{1,0:T(2,128)S(1)}, f32[2,512]{1,0:T(2,128)S(1)}, u32[]{:S(2)}, u32[]{:S(2)}) collective-permute-start(f32[2,512]{1,0:T(2,128)S(1)} %pad_maximum_fusion.refs_4_), channel_id=1, source_target_pairs={{64,0},{72,8},{80,16},{88,24},{96,32},{104,40},{112,48},{120,56},{... | collective-permute-start | bytes 12296 | tf_op jit(solution)/shard_map/ppermute | solution.py:453
  164.7 1.5 copy-start
  164.7 1.7 %copy-start.1 = (bf16[256,1792]{1,0:T(8,128)(2,1)S(1)}, bf16[256,1792]{1,0:T(8,128)(2,1)}, u32[]{:S(2)}) copy-start(bf16[256,1792]{1,0:T(8,128)(2,1)} %gradient.3) | copy-start | bytes 2752516
  164.7 2.0 %copy-start.2 = (bf16[256,1792]{1,0:T(8,128)(2,1)S(1)}, bf16[256,1792]{1,0:T(8,128)(2,1)}, u32[]{:S(2)}) copy-start(bf16[256,1792]{1,0:T(8,128)(2,1)} %weight.1) | copy-start | bytes 2752516
where the time goes:
time: 172 us; the launch traced here: 171 us
  waiting for transfers between devices  61.7 us (36%)
  starting transfers between devices  59 us (34%)
  Pallas kernels  40.8 us (24%)
  local copies, waits for them, and re-layouts  6.14 us (4%)
    pallas_call x1, Pallas kernels, inverse_cholesky(): call(cholesky_kernel, [shape((RANK, RANK))], [VMEM, VMEM, pl.BlockSpec(me...  21 us
    all_to_all x3, starting transfers between devices, over_z(): return lax.all_to_all(a, 'dp', 0, 0, axis_index_groups=Z_GROUPS, tiled=True)  17.3 us
    ppermute x3, waiting for transfers between devices, shards(): mine = [mine] + [lax.ppermute(mine, 'dp', from_y(k)) for k in range(1, NY)]  12.9 us
    ppermute x3, waiting for transfers between devices, shards(): lax.ppermute(both, 'dp', from_y(k))  11 us
    ppermute x3, starting transfers between devices, shards(): lax.ppermute(pairs[k], 'dp', from_z(NZ - 2 * k))  10.1 us
    all_to_all x3, waiting for transfers between devices, over_z(): return lax.all_to_all(a, 'dp', 0, 0, axis_index_groups=Z_GROUPS, tiled=True)  9.96 us
    ppermute x3, waiting for transfers between devices, shards(): lax.ppermute(pair, 'tensor', from_x(k))  9.26 us
    ppermute x3, starting transfers between devices, shards(): mine = [mine] + [lax.ppermute(mine, 'dp', from_y(k)) for k in range(1, NY)]  6.24 us
  transfers between devices with their start and end apart: 29, of which 19 were waited for; matrix products, arithmetic and copies ran while one was open for 1% of the time, Pallas kernels for 16%

commit v1 on v0

--- a/solution.py
+++ b/solution.py
@@ -422,10 +422,10 @@
     xs = [pair] + [lax.ppermute(pair, "tensor", from_x(k)) for k in range(1, NX)]
     mine = (xs[0] + xs[2]) + (xs[1] + xs[3])
     mine = [mine] + [lax.ppermute(mine, "dp", from_y(k)) for k in range(1, NY)]
-    mine, blocks = lax.optimization_barrier((mine, blocks))
 
     gram_given, gram_kept, stacked = gram_halves(mine)
     gram_pair = gram_kept + lax.ppermute(gram_given, "tensor", OTHER_CORE)
+    stacked, blocks = lax.optimization_barrier((stacked, blocks))
     other = lax.ppermute(stacked, "tensor", OTHER_CORE)
 
     right_kept, right_a, right_b, projected = right_sums(stacked, other, blocks)

time: 172 us -> 168 us (0.977)
  local copies, waits for them, and re-layouts: 6.14 us -> 2.83 us
    unnamed x22 -> x14, local copies, waits for them, and re-layouts: 6.14 us -> 2.83 us
  transfers between devices with their start and end apart: 29 -> 29, of which waited for: 19 -> 19; matrix products, arithmetic and copies ran while one was open for 1% -> 1% of each run, Pallas kernels for 16% -> 18%
where the time goes in v1:
time: 168 us
  waiting for transfers between devices  61.5 us (37%)
  starting transfers between devices  59.2 us (35%)
  Pallas kernels  40.8 us (24%)
  local copies, waits for them, and re-layouts  2.83 us (2%)
    pallas_call x1, Pallas kernels, inverse_cholesky(): call(cholesky_kernel, [shape((RANK, RANK))], [VMEM, VMEM, pl.BlockSpec(me...  21 us
    all_to_all x3, starting transfers between devices, over_z(): return lax.all_to_all(a, 'dp', 0, 0, axis_index_groups=Z_GROUPS, tiled=True)  17.3 us
    ppermute x3, waiting for transfers between devices, shards(): mine = [mine] + [lax.ppermute(mine, 'dp', from_y(k)) for k in range(1, NY)]  12.9 us
    ppermute x3, waiting for transfers between devices, shards(): lax.ppermute(both, 'dp', from_y(k))  11 us
    ppermute x3, starting transfers between devices, shards(): lax.ppermute(pairs[k], 'dp', from_z(NZ - 2 * k))  10.1 us
    all_to_all x3, waiting for transfers between devices, over_z(): return lax.all_to_all(a, 'dp', 0, 0, axis_index_groups=Z_GROUPS, tiled=True)  9.96 us
    ppermute x3, waiting for transfers between devices, shards(): lax.ppermute(pair, 'tensor', from_x(k))  9.26 us
    ppermute x3, starting transfers between devices, shards(): mine = [mine] + [lax.ppermute(mine, 'dp', from_y(k)) for k in range(1, NY)]  6.24 us
  transfers between devices with their start and end apart: 29, of which 19 were waited for; matrix products, arithmetic and copies ran while one was open for 1% of the time, Pallas kernels for 18%

profile of v1, /device:TPU:4, one launch (start us, length us, event | category | flops | bytes accessed | tf_op | source)
XLA Modules:
  0.0 167.7 jit_solution(13484974483455642245)
XLA Ops:
  0.6 4.8 %shard_map.67 = (f32[1792,256]{1,0:T(8,128)}, f32[128,512]{1,0:T(8,128)}, f32[128,512]{1,0:T(8,128)}) custom-call(f32[256,1792]{1,0:T(8,128)} %momentum.3, bf16[256,1792]{1,0:T(8,128)(2,1)} %gradient.3, bf16[1792,512]{1,0:T(8,128)(2,1)} %factor.1), custom_call_target="tpu_custom_call" | custom-call | flops 1409286144 | bytes 4587520 | tf_op jit(solution)/shard_map/pallas_call | solution.py:226
  5.5 4.6 %all-to-all-start = ((f32[4,448,256]{2,1,0:T(8,128)}), f32[4,448,256]{2,1,0:T(8,128)S(1)}, u32[]{:S(2)}, u32[]{:S(2)}) async-start(f32[4,448,256]{2,1,0:T(8,128)} %bitcast.15), calls=%async_computation | async-start | bytes 3670016 | tf_op jit(solution)/shard_map/all_to_all | solution.py:420
  10.1 1.5 collective-permute-done
  11.7 1.3 collective-permute-start.3
  13.8 2.7 %collective-permute-start.1 = (f32[128,512]{1,0:T(8,128)S(1)}, f32[128,512]{1,0:T(8,128)S(1)}, u32[]{:S(2)}, u32[]{:S(2)}) collective-permute-start(f32[128,512]{1,0:T(8,128)S(1)} %add.42), channel_id=1, source_target_pairs={{4,0},{5,1},{6,2},{7,3},{0,4},{1,5},{2,6},{3,7},{12,8},{13,9},{14,... | collective-permute-start | bytes 786440 | tf_op jit(solution)/shard_map/ppermute | solution.py:422
  16.4 4.5 %collective-permute-done.3 = f32[128,512]{1,0:T(8,128)S(1)} collective-permute-done((f32[128,512]{1,0:T(8,128)S(1)}, f32[128,512]{1,0:T(8,128)S(1)}, u32[]{:S(2)}, u32[]{:S(2)}) %collective-permute-start.3) | collective-permute-done | bytes 262176 | tf_op jit(solution)/shard_map/ppermute | solution.py:422
  20.9 1.2 collective-permute-done.2
  22.1 3.6 %collective-permute-done.1 = f32[128,512]{1,0:T(8,128)S(1)} collective-permute-done((f32[128,512]{1,0:T(8,128)S(1)}, f32[128,512]{1,0:T(8,128)S(1)}, u32[]{:S(2)}, u32[]{:S(2)}) %collective-permute-start.1) | collective-permute-done | bytes 262176 | tf_op jit(solution)/shard_map/ppermute | solution.py:422
  25.8 2.1 %collective-permute-start.6 = (f32[128,512]{1,0:T(8,128)S(1)}, f32[128,512]{1,0:T(8,128)S(1)}, u32[]{:S(2)}, u32[]{:S(2)}) collective-permute-start(f32[128,512]{1,0:T(8,128)S(1)} %add_add_fusion.refs_0_), channel_id=1, source_target_pairs={{192,0},{200,8},{208,16},{216,24},{224,32},{232,40},{240,48},{248,... | collective-permute-start | bytes 786440 | tf_op jit(solution)/shard_map/ppermute | solution.py:424
  27.9 2.7 %collective-permute-start.5 = (f32[128,512]{1,0:T(8,128)S(1)}, f32[128,512]{1,0:T(8,128)S(1)}, u32[]{:S(2)}, u32[]{:S(2)}) collective-permute-start(f32[128,512]{1,0:T(8,128)S(1)} %add_add_fusion.refs_0_), channel_id=1, source_target_pairs={{128,0},{136,8},{144,16},{152,24},{160,32},{168,40},{176,48},{184,... | collective-permute-start | bytes 786440 | tf_op jit(solution)/shard_map/ppermute | solution.py:424
  30.6 1.5 collective-permute-start.4
  32.0 8.6 %collective-permute-done.6.refs_3_ = f32[128,512]{1,0:T(8,128)S(1)} collective-permute-done((f32[128,512]{1,0:T(8,128)S(1)}, f32[128,512]{1,0:T(8,128)S(1)}, u32[]{:S(2)}, u32[]{:S(2)}) %collective-permute-start.6) | collective-permute-done | bytes 262176 | tf_op jit(solution)/shard_map/ppermute | solution.py:424
  40.6 4.2 %collective-permute-done.5.refs_2_ = f32[128,512]{1,0:T(8,128)S(1)} collective-permute-done((f32[128,512]{1,0:T(8,128)S(1)}, f32[128,512]{1,0:T(8,128)S(1)}, u32[]{:S(2)}, u32[]{:S(2)}) %collective-permute-start.5) | collective-permute-done | bytes 262176 | tf_op jit(solution)/shard_map/ppermute | solution.py:424
  44.9 1.7 %shard_map.68 = (f32[640,128]{1,0:T(8,128)S(1)}, f32[640,128]{1,0:T(8,128)S(1)}, f32[512,512]{1,0:T(8,128)S(1)}) custom-call(f32[128,512]{1,0:T(8,128)S(1)} %add_add_fusion.refs_0_, f32[128,512]{1,0:T(8,128)S(1)} %collective-permute-done.4.refs_1_, f32[128,512]{1,0:T(8,128)S(1)} %collective-permute-done.5.refs_2_, f32[128,512]{1,0:T(8,128)S(1)} %collective-permute-done.6.refs_3_), custom_call_target="tpu_custom_call" | custom-call | flops 1610612736 | bytes 1703936 | tf_op jit(solution)/shard_map/pallas_call | solution.py:257
  47.3 2.6 %collective-permute-done.8 = f32[640,128]{1,0:T(8,128)S(1)} collective-permute-done((f32[640,128]{1,0:T(8,128)S(1)}, f32[640,128]{1,0:T(8,128)S(1)}, u32[]{:S(2)}, u32[]{:S(2)}) %collective-permute-start.8) | collective-permute-done | bytes 327712 | tf_op jit(solution)/shard_map/ppermute | solution.py:427
  50.6 8.5 %all-to-all-start.1 = ((f32[8,80,128]{2,1,0:T(8,128)}), f32[8,80,128]{2,1,0:T(8,128)S(1)}, u32[]{:S(2)}, u32[]{:S(2)}) async-start(f32[8,80,128]{2,1,0:T(8,128)} %bitcast.2), calls=%async_computation.1 | async-start | bytes 655360 | tf_op jit(solution)/shard_map/all_to_all | solution.py:413
  59.1 1.2 copy-done.4
  60.3 5.4 %shard_map.69 = (f32[4,56,512]{2,1,0:T(8,128)S(1)}, f32[4,56,256]{2,1,0:T(8,128)}, f32[4,56,256]{2,1,0:T(8,128)}, f32[256,512]{1,0:T(8,128)S(1)}) custom-call(f32[512,512]{1,0:T(8,128)S(1)} %copy-done.4, f32[512,512]{1,0:T(8,128)} %collective-permute-done.7.other, f32[1792,256]{1,0:T(8,128)S(1)} %bitcast.10), custom_call_target="tpu_custom_call" | custom-call | flops 2818572288 | bytes 4849664 | tf_op jit(solution)/shard_map/pallas_call | solution.py:305
  65.7 2.0 %collective-permute-start.9 = (f32[4,56,256]{2,1,0:T(8,128)}, f32[4,56,256]{2,1,0:T(8,128)S(1)}, u32[]{:S(2)}, u32[]{:S(2)}) collective-permute-start(f32[4,56,256]{2,1,0:T(8,128)} %get-tuple-element.43), channel_id=1, source_target_pairs={{0,8},{8,0},{16,24},{24,16},{32,40},{40,32},{48,56},{56,48},{64,72... | collective-permute-start | bytes 688136 | tf_op jit(solution)/shard_map/ppermute | solution.py:432
  67.7 2.7 %collective-permute-start.10 = (f32[4,56,256]{2,1,0:T(8,128)}, f32[4,56,256]{2,1,0:T(8,128)S(1)}, u32[]{:S(2)}, u32[]{:S(2)}) collective-permute-start(f32[4,56,256]{2,1,0:T(8,128)} %get-tuple-element.44), channel_id=1, source_target_pairs={{0,56},{8,16},{16,8},{24,32},{32,24},{40,48},{48,40},{56,0},{64,12... | collective-permute-start | bytes 688136 | tf_op jit(solution)/shard_map/ppermute | solution.py:433
  70.4 2.3 %all-to-all-done.1 = f32[8,80,128]{2,1,0:T(8,128)S(1)} async-done(((f32[8,80,128]{2,1,0:T(8,128)}), f32[8,80,128]{2,1,0:T(8,128)S(1)}, u32[]{:S(2)}, u32[]{:S(2)}) %all-to-all-start.1) | async-done | bytes 327712 | tf_op jit(solution)/shard_map/all_to_all | solution.py:413
  73.7 3.0 %collective-permute-done.10.from_b = f32[4,56,256]{2,1,0:T(8,128)S(1)} collective-permute-done((f32[4,56,256]{2,1,0:T(8,128)}, f32[4,56,256]{2,1,0:T(8,128)S(1)}, u32[]{:S(2)}, u32[]{:S(2)}) %collective-permute-start.10) | collective-permute-done | bytes 229408 | tf_op jit(solution)/shard_map/ppermute | solution.py:433
  76.6 5.1 %all-to-all-start.2 = ((f32[8,80,128]{2,1,0:T(8,128)}), f32[8,80,128]{2,1,0:T(8,128)S(1)}, u32[]{:S(2)}, u32[]{:S(2)}) async-start(f32[8,80,128]{2,1,0:T(8,128)} %bitcast.4), calls=%async_computation.2 | async-start | bytes 655360 | tf_op jit(solution)/shard_map/all_to_all | solution.py:413
  81.8 3.0 %collective-permute-start.12 = (f32[56,512]{1,0:T(8,128)S(1)}, f32[56,512]{1,0:T(8,128)S(1)}, u32[]{:S(2)}, u32[]{:S(2)}) collective-permute-start(f32[56,512]{1,0:T(8,128)S(1)} %get-tuple-element.50), channel_id=1, source_target_pairs={{48,0},{56,8},{0,16},{8,24},{16,32},{24,40},{32,48},{40,56},{112,6... | collective-permute-start | bytes 344072 | tf_op jit(solution)/shard_map/ppermute | solution.py:437
  84.8 3.6 %collective-permute-start.13 = (f32[56,512]{1,0:T(8,128)S(1)}, f32[56,512]{1,0:T(8,128)S(1)}, u32[]{:S(2)}, u32[]{:S(2)}) collective-permute-start(f32[56,512]{1,0:T(8,128)S(1)} %get-tuple-element.51), channel_id=1, source_target_pairs={{32,0},{40,8},{48,16},{56,24},{0,32},{8,40},{16,48},{24,56},{96,64... | collective-permute-start | bytes 344072 | tf_op jit(solution)/shard_map/ppermute | solution.py:437
  88.4 3.6 %collective-permute-start.14 = (f32[56,512]{1,0:T(8,128)S(1)}, f32[56,512]{1,0:T(8,128)S(1)}, u32[]{:S(2)}, u32[]{:S(2)}) collective-permute-start(f32[56,512]{1,0:T(8,128)S(1)} %get-tuple-element.52), channel_id=1, source_target_pairs={{16,0},{24,8},{32,16},{40,24},{48,32},{56,40},{0,48},{8,56},{80,64... | collective-permute-start | bytes 344072 | tf_op jit(solution)/shard_map/ppermute | solution.py:437
  91.9 4.4 %all-to-all-done.2 = f32[8,80,128]{2,1,0:T(8,128)S(1)} async-done(((f32[8,80,128]{2,1,0:T(8,128)}), f32[8,80,128]{2,1,0:T(8,128)S(1)}, u32[]{:S(2)}, u32[]{:S(2)}) %all-to-all-start.2) | async-done | bytes 327712 | tf_op jit(solution)/shard_map/all_to_all | solution.py:413
  96.3 2.4 %collective-permute-done.12.b = f32[56,512]{1,0:T(8,128)S(1)} collective-permute-done((f32[56,512]{1,0:T(8,128)S(1)}, f32[56,512]{1,0:T(8,128)S(1)}, u32[]{:S(2)}, u32[]{:S(2)}) %collective-permute-start.12) | collective-permute-done | bytes 114720 | tf_op jit(solution)/shard_map/ppermute | solution.py:437
  98.7 3.2 %collective-permute-done.13.c = f32[56,512]{1,0:T(8,128)S(1)} collective-permute-done((f32[56,512]{1,0:T(8,128)S(1)}, f32[56,512]{1,0:T(8,128)S(1)}, u32[]{:S(2)}, u32[]{:S(2)}) %collective-permute-start.13) | collective-permute-done | bytes 114720 | tf_op jit(solution)/shard_map/ppermute | solution.py:437
  101.9 1.0 shard_map.72.after
  102.9 3.8 %all-to-all-start.3 = ((f32[8,56,512]{2,1,0:T(8,128)}), f32[8,56,512]{2,1,0:T(8,128)S(1)}, u32[]{:S(2)}, u32[]{:S(2)}) async-start(f32[8,56,512]{2,1,0:T(8,128)} %bitcast.6), calls=%async_computation.3 | async-start | bytes 1835008 | tf_op jit(solution)/shard_map/all_to_all | solution.py:413
  106.7 21.0 %shard_map.73.inverse = f32[512,512]{1,0:T(8,128)S(1)} custom-call(f32[640,128]{1,0:T(8,128)S(1)} %bitcast.14, f32[640,128]{1,0:T(8,128)S(1)} %collective-permute-done.11.other_ref, f32[448,512]{1,0:T(8,128)} %shard_map.72.after), custom_call_target="tpu_custom_call" | custom-call | flops 10737418240 | bytes 2097152 | tf_op jit(solution)/shard_map/pallas_call | solution.py:132
  127.7 1.1 fusion.basis
  128.8 3.3 %all-to-all-done.3 = f32[8,56,512]{2,1,0:T(8,128)S(1)} async-done(((f32[8,56,512]{2,1,0:T(8,128)}), f32[8,56,512]{2,1,0:T(8,128)S(1)}, u32[]{:S(2)}, u32[]{:S(2)}) %all-to-all-start.3) | async-done | bytes 917536 | tf_op jit(solution)/shard_map/all_to_all | solution.py:413
  132.1 1.8 %shard_map.74 = (f32[448,512]{1,0:T(8,128)S(1)}, f32[1,512]{1,0:T(1,128)S(1)}) custom-call(f32[448,512]{1,0:T(8,128)S(1)} %bitcast.12, f32[512,512]{1,0:T(8,128)S(1)} %shard_map.73.inverse), custom_call_target="tpu_custom_call" | custom-call | flops 1409286144 | bytes 1835008 | tf_op jit(solution)/shard_map/pallas_call | solution.py:354
  134.5 2.1 %collective-permute-start.23 = (f16[448,512]{1,0:T(8,128)(2,1)S(1)}, f16[448,512]{1,0:T(8,128)(2,1)S(1)}, u32[]{:S(2)}, u32[]{:S(2)}) collective-permute-start(f16[448,512]{1,0:T(8,128)(2,1)S(1)} %convert_element_type.15), channel_id=1, source_target_pairs={{128,0},{136,8},{144,16},{152,24},{160,32},{168,40},{176,48},{184,... | collective-permute-start | bytes 1376264 | tf_op jit(solution)/shard_map/ppermute | solution.py:448
  136.6 1.2 collective-permute-start.22
  137.8 1.2 collective-permute-start.17
  139.8 1.6 collective-permute-done.17
  141.4 2.3 %collective-permute-start.15 = (f32[1,512]{1,0:T(1,128)S(1)}, f32[1,512]{1,0:T(1,128)S(1)}, u32[]{:S(2)}, u32[]{:S(2)}) collective-permute-start(f32[1,512]{1,0:T(1,128)S(1)} %get-tuple-element.55), channel_id=1, source_target_pairs={{4,0},{5,1},{6,2},{7,3},{0,4},{1,5},{2,6},{3,7},{12,8},{13,9},{14,... | collective-permute-start | bytes 6152 | tf_op jit(solution)/shard_map/ppermute | solution.py:449
  143.6 2.8 %collective-permute-done.15 = f32[1,512]{1,0:T(1,128)S(1)} collective-permute-done((f32[1,512]{1,0:T(1,128)S(1)}, f32[1,512]{1,0:T(1,128)S(1)}, u32[]{:S(2)}, u32[]{:S(2)}) %collective-permute-start.15) | collective-permute-done | bytes 2080 | tf_op jit(solution)/shard_map/ppermute | solution.py:449
  146.6 1.1 collective-permute-done.18
  147.7 0.9 collective-permute-start.21
  148.6 1.7 collective-permute-start.20
  150.3 7.4 %collective-permute-done.21.refs_7_ = f32[2,512]{1,0:T(2,128)S(1)} collective-permute-done((f32[2,512]{1,0:T(2,128)S(1)}, f32[2,512]{1,0:T(2,128)S(1)}, u32[]{:S(2)}, u32[]{:S(2)}) %collective-permute-start.21) | collective-permute-done | bytes 4128 | tf_op jit(solution)/shard_map/ppermute | solution.py:453
  157.7 3.6 %collective-permute-done.19.refs_5_ = f32[2,512]{1,0:T(2,128)S(1)} collective-permute-done((f32[2,512]{1,0:T(2,128)S(1)}, f32[2,512]{1,0:T(2,128)S(1)}, u32[]{:S(2)}, u32[]{:S(2)}) %collective-permute-start.19) | collective-permute-done | bytes 4128 | tf_op jit(solution)/shard_map/ppermute | solution.py:453
  161.8 1.1 copy-done
  163.4 4.3 %shard_map.75 = (f32[256,1792]{1,0:T(8,128)}, bf16[1792,512]{1,0:T(8,128)(2,1)}, bf16[256,1792]{1,0:T(8,128)(2,1)}) custom-call(f32[256,1792]{1,0:T(8,128)S(1)} %copy-done, bf16[256,1792]{1,0:T(8,128)(2,1)S(1)} %copy-done.1, bf16[256,1792]{1,0:T(8,128)(2,1)S(1)} %copy-done.2, f32[256,512]{1,0:T(8,128)S(1)} %fusion.basis, f32[1,512]{1,0:T(1,128)S(1)} %add_sqrt_fusion.scale, ...), custom_call_target="tpu_custom_call" | custom-call | flops 1879048192 | bytes 7340032 | tf_op jit(solution)/shard_map/pallas_call | solution.py:400
  (46 shorter events, 6.0 us)
Async XLA Ops:
  5.5 4.6 %copy-start.6 = (f32[128,512]{1,0:T(8,128)S(1)}, f32[128,512]{1,0:T(8,128)}, u32[]{:S(2)}) copy-start(f32[128,512]{1,0:T(8,128)} %get-tuple-element.35) | copy-start | bytes 786436
  5.5 6.2 %copy-start.5 = (f32[128,512]{1,0:T(8,128)S(1)}, f32[128,512]{1,0:T(8,128)}, u32[]{:S(2)}) copy-start(f32[128,512]{1,0:T(8,128)} %get-tuple-element.34) | copy-start | bytes 786436
  5.5 41.2 %all-to-all-start = ((f32[4,448,256]{2,1,0:T(8,128)}), f32[4,448,256]{2,1,0:T(8,128)S(1)}, u32[]{:S(2)}, u32[]{:S(2)}) async-start(f32[4,448,256]{2,1,0:T(8,128)} %bitcast.15), calls=%async_computation | async-start | bytes 3670016 | tf_op jit(solution)/shard_map/all_to_all | solution.py:420
  10.1 1.5 collective-permute-start
  11.7 9.2 %collective-permute-start.3 = (f32[128,512]{1,0:T(8,128)S(1)}, f32[128,512]{1,0:T(8,128)S(1)}, u32[]{:S(2)}, u32[]{:S(2)}) collective-permute-start(f32[128,512]{1,0:T(8,128)S(1)} %add.42), channel_id=1, source_target_pairs={{6,0},{7,1},{0,2},{1,3},{2,4},{3,5},{4,6},{5,7},{14,8},{15,9},{8,1... | collective-permute-start | bytes 786440 | tf_op jit(solution)/shard_map/ppermute | solution.py:422
  12.9 9.2 %collective-permute-start.2 = (f32[128,512]{1,0:T(8,128)S(1)}, f32[128,512]{1,0:T(8,128)S(1)}, u32[]{:S(2)}, u32[]{:S(2)}) collective-permute-start(f32[128,512]{1,0:T(8,128)S(1)} %add.42), channel_id=1, source_target_pairs={{2,0},{3,1},{4,2},{5,3},{6,4},{7,5},{0,6},{1,7},{10,8},{11,9},{12,... | collective-permute-start | bytes 786440 | tf_op jit(solution)/shard_map/ppermute | solution.py:422
  13.8 11.9 %collective-permute-start.1 = (f32[128,512]{1,0:T(8,128)S(1)}, f32[128,512]{1,0:T(8,128)S(1)}, u32[]{:S(2)}, u32[]{:S(2)}) collective-permute-start(f32[128,512]{1,0:T(8,128)S(1)} %add.42), channel_id=1, source_target_pairs={{4,0},{5,1},{6,2},{7,3},{0,4},{1,5},{2,6},{3,7},{12,8},{13,9},{14,... | collective-permute-start | bytes 786440 | tf_op jit(solution)/shard_map/ppermute | solution.py:422
  25.8 14.8 %collective-permute-start.6 = (f32[128,512]{1,0:T(8,128)S(1)}, f32[128,512]{1,0:T(8,128)S(1)}, u32[]{:S(2)}, u32[]{:S(2)}) collective-permute-start(f32[128,512]{1,0:T(8,128)S(1)} %add_add_fusion.refs_0_), channel_id=1, source_target_pairs={{192,0},{200,8},{208,16},{216,24},{224,32},{232,40},{240,48},{248,... | collective-permute-start | bytes 786440 | tf_op jit(solution)/shard_map/ppermute | solution.py:424
  27.9 17.0 %collective-permute-start.5 = (f32[128,512]{1,0:T(8,128)S(1)}, f32[128,512]{1,0:T(8,128)S(1)}, u32[]{:S(2)}, u32[]{:S(2)}) collective-permute-start(f32[128,512]{1,0:T(8,128)S(1)} %add_add_fusion.refs_0_), channel_id=1, source_target_pairs={{128,0},{136,8},{144,16},{152,24},{160,32},{168,40},{176,48},{184,... | collective-permute-start | bytes 786440 | tf_op jit(solution)/shard_map/ppermute | solution.py:424
  30.6 14.3 %collective-permute-start.4 = (f32[128,512]{1,0:T(8,128)S(1)}, f32[128,512]{1,0:T(8,128)S(1)}, u32[]{:S(2)}, u32[]{:S(2)}) collective-permute-start(f32[128,512]{1,0:T(8,128)S(1)} %add_add_fusion.refs_0_), channel_id=1, source_target_pairs={{64,0},{72,8},{80,16},{88,24},{96,32},{104,40},{112,48},{120,56},{... | collective-permute-start | bytes 786440 | tf_op jit(solution)/shard_map/ppermute | solution.py:424
  46.6 12.5 %copy-start.3 = (f32[512,512]{1,0:T(8,128)}, f32[512,512]{1,0:T(8,128)S(1)}, u32[]{:S(2)}) copy-start(f32[512,512]{1,0:T(8,128)S(1)} %get-tuple-element.38.mine) | copy-start | bytes 3145732
  46.7 12.4 %collective-permute-start.7 = (f32[512,512]{1,0:T(8,128)S(1)}, f32[512,512]{1,0:T(8,128)}, u32[]{:S(2)}, u32[]{:S(2)}) collective-permute-start(f32[512,512]{1,0:T(8,128)S(1)} %get-tuple-element.38.mine), channel_id=1, source_target_pairs={{1,0},{0,1},{3,2},{2,3},{5,4},{4,5},{7,6},{6,7},{9,8},{8,9},{11,10... | collective-permute-start | bytes 3145736 | tf_op jit(solution)/shard_map/ppermute | solution.py:429
  46.8 3.1 %collective-permute-start.8 = (f32[640,128]{1,0:T(8,128)S(1)}, f32[640,128]{1,0:T(8,128)S(1)}, u32[]{:S(2)}, u32[]{:S(2)}) collective-permute-start(f32[640,128]{1,0:T(8,128)S(1)} %get-tuple-element.42), channel_id=1, source_target_pairs={{1,0},{0,1},{3,2},{2,3},{5,4},{4,5},{7,6},{6,7},{9,8},{8,9},{11,10... | collective-permute-start | bytes 983048 | tf_op jit(solution)/shard_map/ppermute | solution.py:427
  50.6 22.1 %all-to-all-start.1 = ((f32[8,80,128]{2,1,0:T(8,128)}), f32[8,80,128]{2,1,0:T(8,128)S(1)}, u32[]{:S(2)}, u32[]{:S(2)}) async-start(f32[8,80,128]{2,1,0:T(8,128)} %bitcast.2), calls=%async_computation.1 | async-start | bytes 655360 | tf_op jit(solution)/shard_map/all_to_all | solution.py:413
  59.1 1.2 copy-start.4
  65.7 8.0 %collective-permute-start.9 = (f32[4,56,256]{2,1,0:T(8,128)}, f32[4,56,256]{2,1,0:T(8,128)S(1)}, u32[]{:S(2)}, u32[]{:S(2)}) collective-permute-start(f32[4,56,256]{2,1,0:T(8,128)} %get-tuple-element.43), channel_id=1, source_target_pairs={{0,8},{8,0},{16,24},{24,16},{32,40},{40,32},{48,56},{56,48},{64,72... | collective-permute-start | bytes 688136 | tf_op jit(solution)/shard_map/ppermute | solution.py:432
  67.7 8.9 %collective-permute-start.10 = (f32[4,56,256]{2,1,0:T(8,128)}, f32[4,56,256]{2,1,0:T(8,128)S(1)}, u32[]{:S(2)}, u32[]{:S(2)}) collective-permute-start(f32[4,56,256]{2,1,0:T(8,128)} %get-tuple-element.44), channel_id=1, source_target_pairs={{0,56},{8,16},{16,8},{24,32},{32,24},{40,48},{48,40},{56,0},{64,12... | collective-permute-start | bytes 688136 | tf_op jit(solution)/shard_map/ppermute | solution.py:433
  76.6 19.7 %all-to-all-start.2 = ((f32[8,80,128]{2,1,0:T(8,128)}), f32[8,80,128]{2,1,0:T(8,128)S(1)}, u32[]{:S(2)}, u32[]{:S(2)}) async-start(f32[8,80,128]{2,1,0:T(8,128)} %bitcast.4), calls=%async_computation.2 | async-start | bytes 655360 | tf_op jit(solution)/shard_map/all_to_all | solution.py:413
  81.8 16.9 %collective-permute-start.12 = (f32[56,512]{1,0:T(8,128)S(1)}, f32[56,512]{1,0:T(8,128)S(1)}, u32[]{:S(2)}, u32[]{:S(2)}) collective-permute-start(f32[56,512]{1,0:T(8,128)S(1)} %get-tuple-element.50), channel_id=1, source_target_pairs={{48,0},{56,8},{0,16},{8,24},{16,32},{24,40},{32,48},{40,56},{112,6... | collective-permute-start | bytes 344072 | tf_op jit(solution)/shard_map/ppermute | solution.py:437
  84.8 17.1 %collective-permute-start.13 = (f32[56,512]{1,0:T(8,128)S(1)}, f32[56,512]{1,0:T(8,128)S(1)}, u32[]{:S(2)}, u32[]{:S(2)}) collective-permute-start(f32[56,512]{1,0:T(8,128)S(1)} %get-tuple-element.51), channel_id=1, source_target_pairs={{32,0},{40,8},{48,16},{56,24},{0,32},{8,40},{16,48},{24,56},{96,64... | collective-permute-start | bytes 344072 | tf_op jit(solution)/shard_map/ppermute | solution.py:437
  88.4 13.5 %collective-permute-start.14 = (f32[56,512]{1,0:T(8,128)S(1)}, f32[56,512]{1,0:T(8,128)S(1)}, u32[]{:S(2)}, u32[]{:S(2)}) collective-permute-start(f32[56,512]{1,0:T(8,128)S(1)} %get-tuple-element.52), channel_id=1, source_target_pairs={{16,0},{24,8},{32,16},{40,24},{48,32},{56,40},{0,48},{8,56},{80,64... | collective-permute-start | bytes 344072 | tf_op jit(solution)/shard_map/ppermute | solution.py:437
  96.3 10.4 %collective-permute-start.11 = (f32[640,128]{1,0:T(8,128)S(1)}, f32[640,128]{1,0:T(8,128)S(1)}, u32[]{:S(2)}, u32[]{:S(2)}) collective-permute-start(f32[640,128]{1,0:T(8,128)S(1)} %bitcast.13), channel_id=1, source_target_pairs={{1,0},{0,1},{3,2},{2,3},{5,4},{4,5},{7,6},{6,7},{9,8},{8,9},{11,10... | collective-permute-start | bytes 983048 | tf_op jit(solution)/shard_map/ppermute | solution.py:439
  102.9 29.2 %all-to-all-start.3 = ((f32[8,56,512]{2,1,0:T(8,128)}), f32[8,56,512]{2,1,0:T(8,128)S(1)}, u32[]{:S(2)}, u32[]{:S(2)}) async-start(f32[8,56,512]{2,1,0:T(8,128)} %bitcast.6), calls=%async_computation.3 | async-start | bytes 1835008 | tf_op jit(solution)/shard_map/all_to_all | solution.py:413
  133.9 27.3 %collective-permute-start.24 = (f16[448,512]{1,0:T(8,128)(2,1)S(1)}, f16[448,512]{1,0:T(8,128)(2,1)S(1)}, u32[]{:S(2)}, u32[]{:S(2)}) collective-permute-start(f16[448,512]{1,0:T(8,128)(2,1)S(1)} %convert_element_type.15), channel_id=1, source_target_pairs={{192,0},{200,8},{208,16},{216,24},{224,32},{232,40},{240,48},{248,... | collective-permute-start | bytes 1376264 | tf_op jit(solution)/shard_map/ppermute | solution.py:448
  134.5 26.8 %collective-permute-start.23 = (f16[448,512]{1,0:T(8,128)(2,1)S(1)}, f16[448,512]{1,0:T(8,128)(2,1)S(1)}, u32[]{:S(2)}, u32[]{:S(2)}) collective-permute-start(f16[448,512]{1,0:T(8,128)(2,1)S(1)} %convert_element_type.15), channel_id=1, source_target_pairs={{128,0},{136,8},{144,16},{152,24},{160,32},{168,40},{176,48},{184,... | collective-permute-start | bytes 1376264 | tf_op jit(solution)/shard_map/ppermute | solution.py:448
  136.6 24.7 %collective-permute-start.22 = (f16[448,512]{1,0:T(8,128)(2,1)S(1)}, f16[448,512]{1,0:T(8,128)(2,1)S(1)}, u32[]{:S(2)}, u32[]{:S(2)}) collective-permute-start(f16[448,512]{1,0:T(8,128)(2,1)S(1)} %convert_element_type.15), channel_id=1, source_target_pairs={{64,0},{72,8},{80,16},{88,24},{96,32},{104,40},{112,48},{120,56},{... | collective-permute-start | bytes 1376264 | tf_op jit(solution)/shard_map/ppermute | solution.py:448
  137.8 3.6 %collective-permute-start.17 = (f32[1,512]{1,0:T(1,128)S(1)}, f32[1,512]{1,0:T(1,128)S(1)}, u32[]{:S(2)}, u32[]{:S(2)}) collective-permute-start(f32[1,512]{1,0:T(1,128)S(1)} %get-tuple-element.55), channel_id=1, source_target_pairs={{6,0},{7,1},{0,2},{1,3},{2,4},{3,5},{4,6},{5,7},{14,8},{15,9},{8,1... | collective-permute-start | bytes 6152 | tf_op jit(solution)/shard_map/ppermute | solution.py:449
  139.0 4.6 %collective-permute-start.16 = (f32[1,512]{1,0:T(1,128)S(1)}, f32[1,512]{1,0:T(1,128)S(1)}, u32[]{:S(2)}, u32[]{:S(2)}) collective-permute-start(f32[1,512]{1,0:T(1,128)S(1)} %get-tuple-element.55), channel_id=1, source_target_pairs={{2,0},{3,1},{4,2},{5,3},{6,4},{7,5},{0,6},{1,7},{10,8},{11,9},{12,... | collective-permute-start | bytes 6152 | tf_op jit(solution)/shard_map/ppermute | solution.py:449
  141.4 5.1 %collective-permute-start.15 = (f32[1,512]{1,0:T(1,128)S(1)}, f32[1,512]{1,0:T(1,128)S(1)}, u32[]{:S(2)}, u32[]{:S(2)}) collective-permute-start(f32[1,512]{1,0:T(1,128)S(1)} %get-tuple-element.55), channel_id=1, source_target_pairs={{4,0},{5,1},{6,2},{7,3},{0,4},{1,5},{2,6},{3,7},{12,8},{13,9},{14,... | collective-permute-start | bytes 6152 | tf_op jit(solution)/shard_map/ppermute | solution.py:449
  146.5 1.2 collective-permute-start.18
  147.7 9.9 %collective-permute-start.21 = (f32[2,512]{1,0:T(2,128)S(1)}, f32[2,512]{1,0:T(2,128)S(1)}, u32[]{:S(2)}, u32[]{:S(2)}) collective-permute-start(f32[2,512]{1,0:T(2,128)S(1)} %pad_maximum_fusion.refs_4_), channel_id=1, source_target_pairs={{192,0},{200,8},{208,16},{216,24},{224,32},{232,40},{240,48},{248,... | collective-permute-start | bytes 12296 | tf_op jit(solution)/shard_map/ppermute | solution.py:453
  148.6 9.0 %collective-permute-start.20 = (f32[2,512]{1,0:T(2,128)S(1)}, f32[2,512]{1,0:T(2,128)S(1)}, u32[]{:S(2)}, u32[]{:S(2)}) collective-permute-start(f32[2,512]{1,0:T(2,128)S(1)} %pad_maximum_fusion.refs_4_), channel_id=1, source_target_pairs={{128,0},{136,8},{144,16},{152,24},{160,32},{168,40},{176,48},{184,... | collective-permute-start | bytes 12296 | tf_op jit(solution)/shard_map/ppermute | solution.py:453
  157.7 3.6 %collective-permute-start.19 = (f32[2,512]{1,0:T(2,128)S(1)}, f32[2,512]{1,0:T(2,128)S(1)}, u32[]{:S(2)}, u32[]{:S(2)}) collective-permute-start(f32[2,512]{1,0:T(2,128)S(1)} %pad_maximum_fusion.refs_4_), channel_id=1, source_target_pairs={{64,0},{72,8},{80,16},{88,24},{96,32},{104,40},{112,48},{120,56},{... | collective-permute-start | bytes 12296 | tf_op jit(solution)/shard_map/ppermute | solution.py:453
  161.4 1.5 copy-start
  161.4 1.7 %copy-start.1 = (bf16[256,1792]{1,0:T(8,128)(2,1)S(1)}, bf16[256,1792]{1,0:T(8,128)(2,1)}, u32[]{:S(2)}) copy-start(bf16[256,1792]{1,0:T(8,128)(2,1)} %gradient.3) | copy-start | bytes 2752516
  161.4 2.0 %copy-start.2 = (bf16[256,1792]{1,0:T(8,128)(2,1)S(1)}, bf16[256,1792]{1,0:T(8,128)(2,1)}, u32[]{:S(2)}) copy-start(bf16[256,1792]{1,0:T(8,128)(2,1)} %weight.1) | copy-start | bytes 2752516

commit v2 on v1

--- a/solution.py
+++ b/solution.py
@@ -342,23 +342,28 @@
     return jnp.sqrt(jnp.maximum(squares / count, 1e-30))
 
 
-def normal_kernel(right0, inverse, sent, squares):
-    right = dot_t(right0[...], inverse[...])
+def normal_kernel(right0, projected, inverse, sent, squares, basis, stacked):
+    quarter = right0.shape[0]
+    stacked[:quarter, :] = right0[...]
+    stacked[quarter:, :] = projected[...]
+    both = dot_t(stacked[...], inverse[...])
+    right = both[:quarter]
     sums = jnp.sum(right * right, axis=0, keepdims=True)
     squares[...] = sums
-    sent[...] = right / level(sums, right.shape[0])
-
-
-def normalised(right0, inverse):
-    quarter = right0.shape[0]
+    sent[...] = right / level(sums, quarter)
+    basis[...] = both[quarter:]
+
+
+def normalised(right0, projected, inverse):
+    quarter, rows = right0.shape[0], projected.shape[0]
     return call(
         normal_kernel,
-        [shape((quarter, RANK)), shape((1, RANK))],
-        [VMEM, VMEM],
-        [],
-        12 * quarter * RANK * RANK,
-        8 * quarter * RANK,
-    )(right0, inverse)
+        [shape((quarter, RANK)), shape((1, RANK)), shape((rows, RANK))],
+        [VMEM] * 3,
+        [pltpu.VMEM((quarter + rows, RANK), f32)],
+        12 * (quarter + rows) * RANK * RANK,
+        8 * (quarter + rows) * RANK,
+    )(right0, projected, inverse)
 
 
 def update_kernel(momentum, gradient, weight, basis, scale, *refs):
@@ -441,9 +446,7 @@
     inverse = inverse_cholesky(gram_half, gram_other, right0)
     right0 = over_z(right0)
 
-    basis = dot_t(projected, inverse)
-    basis, right0 = lax.optimization_barrier((basis, right0))
-    sent, squares = normalised(right0, inverse)
+    sent, squares, basis = normalised(right0, projected, inverse)
     sent = sent.astype(jnp.float16)
     sent_y = [sent] + [lax.ppermute(sent, "dp", from_y(k)) for k in range(1, NY)]
     squares_x = [squares] + [lax.ppermute(squares, "tensor", from_x(k)) for k in range(1, NX)]

time: 168 us -> 169 us (level)
    all_to_all x3, waiting for transfers between devices: 9.96 us -> 5.1 us  [over_z(): return lax.all_to_all(a, 'dp', 0, 0, axis_index_groups=Z_GROUPS, tiled=True)]
    ppermute x3, waiting for transfers between devices: 5.61 us -> 9.97 us  [shards(): lax.ppermute(pairs[k], 'dp', from_z(NZ - 2 * k))]
    unnamed x14 -> x18, local copies, waits for them, and re-layouts: 2.83 us -> 3.63 us
  transfers between devices with their start and end apart: 29 -> 29, of which waited for: 19 -> 18; matrix products, arithmetic and copies ran while one was open for 1% -> 1% of each run, Pallas kernels for 18% -> 17%
where the time goes in v2:
time: 169 us; the launch traced here: 168 us
  waiting for transfers between devices  62.1 us (37%)
  starting transfers between devices  59.5 us (35%)
  Pallas kernels  40.8 us (24%)
  local copies, waits for them, and re-layouts  3.63 us (2%)
    pallas_call x1, Pallas kernels, inverse_cholesky(): call(cholesky_kernel, [shape((RANK, RANK))], [VMEM, VMEM, pl.BlockSpec(me...  21 us
    all_to_all x3, starting transfers between devices, over_z(): return lax.all_to_all(a, 'dp', 0, 0, axis_index_groups=Z_GROUPS, tiled=True)  17.1 us
    ppermute x3, waiting for transfers between devices, shards(): mine = [mine] + [lax.ppermute(mine, 'dp', from_y(k)) for k in range(1, NY)]  12.9 us
    ppermute x3, waiting for transfers between devices, shards(): lax.ppermute(both, 'dp', from_y(k))  10.7 us
    ppermute x3, starting transfers between devices, shards(): lax.ppermute(pairs[k], 'dp', from_z(NZ - 2 * k))  10.1 us
    ppermute x3, waiting for transfers between devices, shards(): lax.ppermute(pairs[k], 'dp', from_z(NZ - 2 * k))  9.97 us
    ppermute x3, waiting for transfers between devices, shards(): lax.ppermute(pair, 'tensor', from_x(k))  9.26 us
    ppermute x3, starting transfers between devices, shards(): mine = [mine] + [lax.ppermute(mine, 'dp', from_y(k)) for k in range(1, NY)]  6.24 us
  transfers between devices with their start and end apart: 29, of which 18 were waited for; matrix products, arithmetic and copies ran while one was open for 1% of the time, Pallas kernels for 17%

profile of v2, /device:TPU:4, one launch (start us, length us, event | category | flops | bytes accessed | tf_op | source)
XLA Modules:
  0.0 168.3 jit_solution(13699718466005630239)
XLA Ops:
  0.6 4.8 %shard_map.67 = (f32[1792,256]{1,0:T(8,128)}, f32[128,512]{1,0:T(8,128)}, f32[128,512]{1,0:T(8,128)}) custom-call(f32[256,1792]{1,0:T(8,128)} %momentum.3, bf16[256,1792]{1,0:T(8,128)(2,1)} %gradient.3, bf16[1792,512]{1,0:T(8,128)(2,1)} %factor.1), custom_call_target="tpu_custom_call" | custom-call | flops 1409286144 | bytes 4587520 | tf_op jit(solution)/shard_map/pallas_call | solution.py:226
  5.5 4.6 %all-to-all-start = ((f32[4,448,256]{2,1,0:T(8,128)}), f32[4,448,256]{2,1,0:T(8,128)S(1)}, u32[]{:S(2)}, u32[]{:S(2)}) async-start(f32[4,448,256]{2,1,0:T(8,128)} %bitcast.13), calls=%async_computation | async-start | bytes 3670016 | tf_op jit(solution)/shard_map/all_to_all | solution.py:425
  10.1 1.5 collective-permute-done
  11.7 1.3 collective-permute-start.3
  12.9 0.8 collective-permute-start.2
  13.8 2.7 %collective-permute-start.1 = (f32[128,512]{1,0:T(8,128)S(1)}, f32[128,512]{1,0:T(8,128)S(1)}, u32[]{:S(2)}, u32[]{:S(2)}) collective-permute-start(f32[128,512]{1,0:T(8,128)S(1)} %add.42), channel_id=1, source_target_pairs={{4,0},{5,1},{6,2},{7,3},{0,4},{1,5},{2,6},{3,7},{12,8},{13,9},{14,... | collective-permute-start | bytes 786440 | tf_op jit(solution)/shard_map/ppermute | solution.py:427
  16.4 4.5 %collective-permute-done.3 = f32[128,512]{1,0:T(8,128)S(1)} collective-permute-done((f32[128,512]{1,0:T(8,128)S(1)}, f32[128,512]{1,0:T(8,128)S(1)}, u32[]{:S(2)}, u32[]{:S(2)}) %collective-permute-start.3) | collective-permute-done | bytes 262176 | tf_op jit(solution)/shard_map/ppermute | solution.py:427
  20.9 1.2 collective-permute-done.2
  22.1 3.6 %collective-permute-done.1 = f32[128,512]{1,0:T(8,128)S(1)} collective-permute-done((f32[128,512]{1,0:T(8,128)S(1)}, f32[128,512]{1,0:T(8,128)S(1)}, u32[]{:S(2)}, u32[]{:S(2)}) %collective-permute-start.1) | collective-permute-done | bytes 262176 | tf_op jit(solution)/shard_map/ppermute | solution.py:427
  25.8 2.1 %collective-permute-start.6 = (f32[128,512]{1,0:T(8,128)S(1)}, f32[128,512]{1,0:T(8,128)S(1)}, u32[]{:S(2)}, u32[]{:S(2)}) collective-permute-start(f32[128,512]{1,0:T(8,128)S(1)} %add_add_fusion.refs_0_), channel_id=1, source_target_pairs={{192,0},{200,8},{208,16},{216,24},{224,32},{232,40},{240,48},{248,... | collective-permute-start | bytes 786440 | tf_op jit(solution)/shard_map/ppermute | solution.py:429
  27.9 2.7 %collective-permute-start.5 = (f32[128,512]{1,0:T(8,128)S(1)}, f32[128,512]{1,0:T(8,128)S(1)}, u32[]{:S(2)}, u32[]{:S(2)}) collective-permute-start(f32[128,512]{1,0:T(8,128)S(1)} %add_add_fusion.refs_0_), channel_id=1, source_target_pairs={{128,0},{136,8},{144,16},{152,24},{160,32},{168,40},{176,48},{184,... | collective-permute-start | bytes 786440 | tf_op jit(solution)/shard_map/ppermute | solution.py:429
  30.6 1.5 collective-permute-start.4
  32.0 8.6 %collective-permute-done.6.refs_3_ = f32[128,512]{1,0:T(8,128)S(1)} collective-permute-done((f32[128,512]{1,0:T(8,128)S(1)}, f32[128,512]{1,0:T(8,128)S(1)}, u32[]{:S(2)}, u32[]{:S(2)}) %collective-permute-start.6) | collective-permute-done | bytes 262176 | tf_op jit(solution)/shard_map/ppermute | solution.py:429
  40.6 4.2 %collective-permute-done.5.refs_2_ = f32[128,512]{1,0:T(8,128)S(1)} collective-permute-done((f32[128,512]{1,0:T(8,128)S(1)}, f32[128,512]{1,0:T(8,128)S(1)}, u32[]{:S(2)}, u32[]{:S(2)}) %collective-permute-start.5) | collective-permute-done | bytes 262176 | tf_op jit(solution)/shard_map/ppermute | solution.py:429
  44.9 1.7 %shard_map.68 = (f32[640,128]{1,0:T(8,128)S(1)}, f32[640,128]{1,0:T(8,128)S(1)}, f32[512,512]{1,0:T(8,128)S(1)}) custom-call(f32[128,512]{1,0:T(8,128)S(1)} %add_add_fusion.refs_0_, f32[128,512]{1,0:T(8,128)S(1)} %collective-permute-done.4.refs_1_, f32[128,512]{1,0:T(8,128)S(1)} %collective-permute-done.5.refs_2_, f32[128,512]{1,0:T(8,128)S(1)} %collective-permute-done.6.refs_3_), custom_call_target="tpu_custom_call" | custom-call | flops 1610612736 | bytes 1703936 | tf_op jit(solution)/shard_map/pallas_call | solution.py:257
  47.3 2.6 %collective-permute-done.8 = f32[640,128]{1,0:T(8,128)S(1)} collective-permute-done((f32[640,128]{1,0:T(8,128)S(1)}, f32[640,128]{1,0:T(8,128)S(1)}, u32[]{:S(2)}, u32[]{:S(2)}) %collective-permute-start.8) | collective-permute-done | bytes 327712 | tf_op jit(solution)/shard_map/ppermute | solution.py:432
  50.6 8.5 %all-to-all-start.1 = ((f32[8,80,128]{2,1,0:T(8,128)}), f32[8,80,128]{2,1,0:T(8,128)S(1)}, u32[]{:S(2)}, u32[]{:S(2)}) async-start(f32[8,80,128]{2,1,0:T(8,128)} %bitcast.2), calls=%async_computation.1 | async-start | bytes 655360 | tf_op jit(solution)/shard_map/all_to_all | solution.py:418
  59.1 1.2 copy-done.4
  60.3 4.6 %shard_map.69 = (f32[4,56,512]{2,1,0:T(8,128)S(1)}, f32[4,56,256]{2,1,0:T(8,128)S(1)}, f32[4,56,256]{2,1,0:T(8,128)S(1)}, f32[256,512]{1,0:T(8,128)S(1)}) custom-call(f32[512,512]{1,0:T(8,128)S(1)} %copy-done.4, f32[512,512]{1,0:T(8,128)} %collective-permute-done.7.other, f32[1792,256]{1,0:T(8,128)S(1)} %bitcast.8), custom_call_target="tpu_custom_call" | custom-call | flops 2818572288 | bytes 4849664 | tf_op jit(solution)/shard_map/pallas_call | solution.py:305
  65.7 2.0 %collective-permute-start.9 = (f32[4,56,256]{2,1,0:T(8,128)S(1)}, f32[4,56,256]{2,1,0:T(8,128)S(1)}, u32[]{:S(2)}, u32[]{:S(2)}) collective-permute-start(f32[4,56,256]{2,1,0:T(8,128)S(1)} %get-tuple-element.42), channel_id=1, source_target_pairs={{0,8},{8,0},{16,24},{24,16},{32,40},{40,32},{48,56},{56,48},{64,72... | collective-permute-start | bytes 688136 | tf_op jit(solution)/shard_map/ppermute | solution.py:437
  67.8 2.7 %collective-permute-start.10 = (f32[4,56,256]{2,1,0:T(8,128)S(1)}, f32[4,56,256]{2,1,0:T(8,128)S(1)}, u32[]{:S(2)}, u32[]{:S(2)}) collective-permute-start(f32[4,56,256]{2,1,0:T(8,128)S(1)} %get-tuple-element.43), channel_id=1, source_target_pairs={{0,56},{8,16},{16,8},{24,32},{32,24},{40,48},{48,40},{56,0},{64,12... | collective-permute-start | bytes 688136 | tf_op jit(solution)/shard_map/ppermute | solution.py:438
  70.4 2.5 %all-to-all-done.1 = f32[8,80,128]{2,1,0:T(8,128)S(1)} async-done(((f32[8,80,128]{2,1,0:T(8,128)}), f32[8,80,128]{2,1,0:T(8,128)S(1)}, u32[]{:S(2)}, u32[]{:S(2)}) %all-to-all-start.1) | async-done | bytes 327712 | tf_op jit(solution)/shard_map/all_to_all | solution.py:418
  73.7 2.8 %collective-permute-done.10.from_b = f32[4,56,256]{2,1,0:T(8,128)S(1)} collective-permute-done((f32[4,56,256]{2,1,0:T(8,128)S(1)}, f32[4,56,256]{2,1,0:T(8,128)S(1)}, u32[]{:S(2)}, u32[]{:S(2)}) %collective-permute-start.10) | collective-permute-done | bytes 229408 | tf_op jit(solution)/shard_map/ppermute | solution.py:438
  76.5 5.1 %all-to-all-start.3 = ((f32[8,80,128]{2,1,0:T(8,128)}), f32[8,80,128]{2,1,0:T(8,128)S(1)}, u32[]{:S(2)}, u32[]{:S(2)}) async-start(f32[8,80,128]{2,1,0:T(8,128)} %bitcast.6), calls=%async_computation.3 | async-start | bytes 655360 | tf_op jit(solution)/shard_map/all_to_all | solution.py:418
  81.6 3.0 %collective-permute-start.11 = (f32[56,512]{1,0:T(8,128)S(1)}, f32[56,512]{1,0:T(8,128)S(1)}, u32[]{:S(2)}, u32[]{:S(2)}) collective-permute-start(f32[56,512]{1,0:T(8,128)S(1)} %get-tuple-element.47), channel_id=1, source_target_pairs={{48,0},{56,8},{0,16},{8,24},{16,32},{24,40},{32,48},{40,56},{112,6... | collective-permute-start | bytes 344072 | tf_op jit(solution)/shard_map/ppermute | solution.py:442
  84.6 3.6 %collective-permute-start.12 = (f32[56,512]{1,0:T(8,128)S(1)}, f32[56,512]{1,0:T(8,128)S(1)}, u32[]{:S(2)}, u32[]{:S(2)}) collective-permute-start(f32[56,512]{1,0:T(8,128)S(1)} %get-tuple-element.48), channel_id=1, source_target_pairs={{32,0},{40,8},{48,16},{56,24},{0,32},{8,40},{16,48},{24,56},{96,64... | collective-permute-start | bytes 344072 | tf_op jit(solution)/shard_map/ppermute | solution.py:442
  88.2 3.6 %collective-permute-start.13 = (f32[56,512]{1,0:T(8,128)S(1)}, f32[56,512]{1,0:T(8,128)S(1)}, u32[]{:S(2)}, u32[]{:S(2)}) collective-permute-start(f32[56,512]{1,0:T(8,128)S(1)} %get-tuple-element.49), channel_id=1, source_target_pairs={{16,0},{24,8},{32,16},{40,24},{48,32},{56,40},{0,48},{8,56},{80,64... | collective-permute-start | bytes 344072 | tf_op jit(solution)/shard_map/ppermute | solution.py:442
  91.8 6.8 %collective-permute-done.11.b = f32[56,512]{1,0:T(8,128)S(1)} collective-permute-done((f32[56,512]{1,0:T(8,128)S(1)}, f32[56,512]{1,0:T(8,128)S(1)}, u32[]{:S(2)}, u32[]{:S(2)}) %collective-permute-start.11) | collective-permute-done | bytes 114720 | tf_op jit(solution)/shard_map/ppermute | solution.py:442
  98.6 3.2 %collective-permute-done.12.c = f32[56,512]{1,0:T(8,128)S(1)} collective-permute-done((f32[56,512]{1,0:T(8,128)S(1)}, f32[56,512]{1,0:T(8,128)S(1)}, u32[]{:S(2)}, u32[]{:S(2)}) %collective-permute-start.12) | collective-permute-done | bytes 114720 | tf_op jit(solution)/shard_map/ppermute | solution.py:442
  101.7 1.0 shard_map.72.after
  102.7 3.6 %all-to-all-start.2 = ((f32[8,56,512]{2,1,0:T(8,128)}), f32[8,56,512]{2,1,0:T(8,128)S(1)}, u32[]{:S(2)}, u32[]{:S(2)}) async-start(f32[8,56,512]{2,1,0:T(8,128)} %bitcast.4), calls=%async_computation.2 | async-start | bytes 1835008 | tf_op jit(solution)/shard_map/all_to_all | solution.py:418
  106.6 1.6 collective-permute-done.14.other_ref
  108.2 21.0 %shard_map.73.inverse = f32[512,512]{1,0:T(8,128)S(1)} custom-call(f32[640,128]{1,0:T(8,128)S(1)} %bitcast.12, f32[640,128]{1,0:T(8,128)S(1)} %collective-permute-done.14.other_ref, f32[448,512]{1,0:T(8,128)} %shard_map.72.after), custom_call_target="tpu_custom_call" | custom-call | flops 10737418240 | bytes 2097152 | tf_op jit(solution)/shard_map/pallas_call | solution.py:132
  129.3 2.6 %all-to-all-done.2 = f32[8,56,512]{2,1,0:T(8,128)S(1)} async-done(((f32[8,56,512]{2,1,0:T(8,128)}), f32[8,56,512]{2,1,0:T(8,128)S(1)}, u32[]{:S(2)}, u32[]{:S(2)}) %all-to-all-start.2) | async-done | bytes 917536 | tf_op jit(solution)/shard_map/all_to_all | solution.py:418
  131.9 2.5 %shard_map.74 = (f32[448,512]{1,0:T(8,128)S(1)}, f32[1,512]{1,0:T(1,128)S(1)}, f32[256,512]{1,0:T(8,128)S(1)}) custom-call(f32[448,512]{1,0:T(8,128)S(1)} %bitcast.10, f32[256,512]{1,0:T(8,128)S(1)} %copy-done.6, f32[512,512]{1,0:T(8,128)S(1)} %shard_map.73.inverse), custom_call_target="tpu_custom_call" | custom-call | flops 2214592512 | bytes 2883584 | tf_op jit(solution)/shard_map/pallas_call | solution.py:359
  135.1 2.1 %collective-permute-start.23 = (f16[448,512]{1,0:T(8,128)(2,1)S(1)}, f16[448,512]{1,0:T(8,128)(2,1)S(1)}, u32[]{:S(2)}, u32[]{:S(2)}) collective-permute-start(f16[448,512]{1,0:T(8,128)(2,1)S(1)} %convert_element_type.15), channel_id=1, source_target_pairs={{128,0},{136,8},{144,16},{152,24},{160,32},{168,40},{176,48},{184,... | collective-permute-start | bytes 1376264 | tf_op jit(solution)/shard_map/ppermute | solution.py:451
  137.2 1.2 collective-permute-start.22
  138.4 1.2 collective-permute-start.17
  140.4 1.6 collective-permute-done.17
  142.0 2.2 %collective-permute-start.15 = (f32[1,512]{1,0:T(1,128)S(1)}, f32[1,512]{1,0:T(1,128)S(1)}, u32[]{:S(2)}, u32[]{:S(2)}) collective-permute-start(f32[1,512]{1,0:T(1,128)S(1)} %get-tuple-element.53), channel_id=1, source_target_pairs={{4,0},{5,1},{6,2},{7,3},{0,4},{1,5},{2,6},{3,7},{12,8},{13,9},{14,... | collective-permute-start | bytes 6152 | tf_op jit(solution)/shard_map/ppermute | solution.py:452
  144.2 2.8 %collective-permute-done.15 = f32[1,512]{1,0:T(1,128)S(1)} collective-permute-done((f32[1,512]{1,0:T(1,128)S(1)}, f32[1,512]{1,0:T(1,128)S(1)}, u32[]{:S(2)}, u32[]{:S(2)}) %collective-permute-start.15) | collective-permute-done | bytes 2080 | tf_op jit(solution)/shard_map/ppermute | solution.py:452
  147.4 1.1 collective-permute-done.18
  148.6 0.9 collective-permute-start.21
  149.5 1.7 collective-permute-start.20
  151.1 7.1 %collective-permute-done.21.refs_7_ = f32[2,512]{1,0:T(2,128)S(1)} collective-permute-done((f32[2,512]{1,0:T(2,128)S(1)}, f32[2,512]{1,0:T(2,128)S(1)}, u32[]{:S(2)}, u32[]{:S(2)}) %collective-permute-start.21) | collective-permute-done | bytes 4128 | tf_op jit(solution)/shard_map/ppermute | solution.py:456
  158.3 3.6 %collective-permute-done.19.refs_5_ = f32[2,512]{1,0:T(2,128)S(1)} collective-permute-done((f32[2,512]{1,0:T(2,128)S(1)}, f32[2,512]{1,0:T(2,128)S(1)}, u32[]{:S(2)}, u32[]{:S(2)}) %collective-permute-start.19) | collective-permute-done | bytes 4128 | tf_op jit(solution)/shard_map/ppermute | solution.py:456
  162.4 1.1 copy-done
  164.0 4.3 %shard_map.75 = (f32[256,1792]{1,0:T(8,128)}, bf16[1792,512]{1,0:T(8,128)(2,1)}, bf16[256,1792]{1,0:T(8,128)(2,1)}) custom-call(f32[256,1792]{1,0:T(8,128)S(1)} %copy-done, bf16[256,1792]{1,0:T(8,128)(2,1)S(1)} %copy-done.1, bf16[256,1792]{1,0:T(8,128)(2,1)S(1)} %copy-done.2, f32[256,512]{1,0:T(8,128)S(1)} %get-tuple-element.52.basis, ...), custom_call_target="tpu_custom_call" | custom-call | flops 1879048192 | bytes 7340032 | tf_op jit(solution)/shard_map/pallas_call | solution.py:405
  (49 shorter events, 6.3 us)
Async XLA Ops:
  5.5 4.6 %copy-start.8 = (f32[128,512]{1,0:T(8,128)S(1)}, f32[128,512]{1,0:T(8,128)}, u32[]{:S(2)}) copy-start(f32[128,512]{1,0:T(8,128)} %get-tuple-element.34) | copy-start | bytes 786436
  5.5 6.2 %copy-start.7 = (f32[128,512]{1,0:T(8,128)S(1)}, f32[128,512]{1,0:T(8,128)}, u32[]{:S(2)}) copy-start(f32[128,512]{1,0:T(8,128)} %get-tuple-element.33) | copy-start | bytes 786436
  5.5 41.2 %all-to-all-start = ((f32[4,448,256]{2,1,0:T(8,128)}), f32[4,448,256]{2,1,0:T(8,128)S(1)}, u32[]{:S(2)}, u32[]{:S(2)}) async-start(f32[4,448,256]{2,1,0:T(8,128)} %bitcast.13), calls=%async_computation | async-start | bytes 3670016 | tf_op jit(solution)/shard_map/all_to_all | solution.py:425
  10.1 1.5 collective-permute-start
  11.7 9.2 %collective-permute-start.3 = (f32[128,512]{1,0:T(8,128)S(1)}, f32[128,512]{1,0:T(8,128)S(1)}, u32[]{:S(2)}, u32[]{:S(2)}) collective-permute-start(f32[128,512]{1,0:T(8,128)S(1)} %add.42), channel_id=1, source_target_pairs={{6,0},{7,1},{0,2},{1,3},{2,4},{3,5},{4,6},{5,7},{14,8},{15,9},{8,1... | collective-permute-start | bytes 786440 | tf_op jit(solution)/shard_map/ppermute | solution.py:427
  12.9 9.2 %collective-permute-start.2 = (f32[128,512]{1,0:T(8,128)S(1)}, f32[128,512]{1,0:T(8,128)S(1)}, u32[]{:S(2)}, u32[]{:S(2)}) collective-permute-start(f32[128,512]{1,0:T(8,128)S(1)} %add.42), channel_id=1, source_target_pairs={{2,0},{3,1},{4,2},{5,3},{6,4},{7,5},{0,6},{1,7},{10,8},{11,9},{12,... | collective-permute-start | bytes 786440 | tf_op jit(solution)/shard_map/ppermute | solution.py:427
  13.8 11.9 %collective-permute-start.1 = (f32[128,512]{1,0:T(8,128)S(1)}, f32[128,512]{1,0:T(8,128)S(1)}, u32[]{:S(2)}, u32[]{:S(2)}) collective-permute-start(f32[128,512]{1,0:T(8,128)S(1)} %add.42), channel_id=1, source_target_pairs={{4,0},{5,1},{6,2},{7,3},{0,4},{1,5},{2,6},{3,7},{12,8},{13,9},{14,... | collective-permute-start | bytes 786440 | tf_op jit(solution)/shard_map/ppermute | solution.py:427
  25.8 14.8 %collective-permute-start.6 = (f32[128,512]{1,0:T(8,128)S(1)}, f32[128,512]{1,0:T(8,128)S(1)}, u32[]{:S(2)}, u32[]{:S(2)}) collective-permute-start(f32[128,512]{1,0:T(8,128)S(1)} %add_add_fusion.refs_0_), channel_id=1, source_target_pairs={{192,0},{200,8},{208,16},{216,24},{224,32},{232,40},{240,48},{248,... | collective-permute-start | bytes 786440 | tf_op jit(solution)/shard_map/ppermute | solution.py:429
  27.9 17.0 %collective-permute-start.5 = (f32[128,512]{1,0:T(8,128)S(1)}, f32[128,512]{1,0:T(8,128)S(1)}, u32[]{:S(2)}, u32[]{:S(2)}) collective-permute-start(f32[128,512]{1,0:T(8,128)S(1)} %add_add_fusion.refs_0_), channel_id=1, source_target_pairs={{128,0},{136,8},{144,16},{152,24},{160,32},{168,40},{176,48},{184,... | collective-permute-start | bytes 786440 | tf_op jit(solution)/shard_map/ppermute | solution.py:429
  30.6 14.3 %collective-permute-start.4 = (f32[128,512]{1,0:T(8,128)S(1)}, f32[128,512]{1,0:T(8,128)S(1)}, u32[]{:S(2)}, u32[]{:S(2)}) collective-permute-start(f32[128,512]{1,0:T(8,128)S(1)} %add_add_fusion.refs_0_), channel_id=1, source_target_pairs={{64,0},{72,8},{80,16},{88,24},{96,32},{104,40},{112,48},{120,56},{... | collective-permute-start | bytes 786440 | tf_op jit(solution)/shard_map/ppermute | solution.py:429
  46.6 12.5 %copy-start.3 = (f32[512,512]{1,0:T(8,128)}, f32[512,512]{1,0:T(8,128)S(1)}, u32[]{:S(2)}) copy-start(f32[512,512]{1,0:T(8,128)S(1)} %get-tuple-element.37.mine) | copy-start | bytes 3145732
  46.7 12.4 %collective-permute-start.7 = (f32[512,512]{1,0:T(8,128)S(1)}, f32[512,512]{1,0:T(8,128)}, u32[]{:S(2)}, u32[]{:S(2)}) collective-permute-start(f32[512,512]{1,0:T(8,128)S(1)} %get-tuple-element.37.mine), channel_id=1, source_target_pairs={{1,0},{0,1},{3,2},{2,3},{5,4},{4,5},{7,6},{6,7},{9,8},{8,9},{11,10... | collective-permute-start | bytes 3145736 | tf_op jit(solution)/shard_map/ppermute | solution.py:434
  46.8 3.1 %collective-permute-start.8 = (f32[640,128]{1,0:T(8,128)S(1)}, f32[640,128]{1,0:T(8,128)S(1)}, u32[]{:S(2)}, u32[]{:S(2)}) collective-permute-start(f32[640,128]{1,0:T(8,128)S(1)} %get-tuple-element.41), channel_id=1, source_target_pairs={{1,0},{0,1},{3,2},{2,3},{5,4},{4,5},{7,6},{6,7},{9,8},{8,9},{11,10... | collective-permute-start | bytes 983048 | tf_op jit(solution)/shard_map/ppermute | solution.py:432
  50.6 22.3 %all-to-all-start.1 = ((f32[8,80,128]{2,1,0:T(8,128)}), f32[8,80,128]{2,1,0:T(8,128)S(1)}, u32[]{:S(2)}, u32[]{:S(2)}) async-start(f32[8,80,128]{2,1,0:T(8,128)} %bitcast.2), calls=%async_computation.1 | async-start | bytes 655360 | tf_op jit(solution)/shard_map/all_to_all | solution.py:418
  59.1 1.2 copy-start.4
  64.9 0.8 copy-start.5
  65.7 8.0 %collective-permute-start.9 = (f32[4,56,256]{2,1,0:T(8,128)S(1)}, f32[4,56,256]{2,1,0:T(8,128)S(1)}, u32[]{:S(2)}, u32[]{:S(2)}) collective-permute-start(f32[4,56,256]{2,1,0:T(8,128)S(1)} %get-tuple-element.42), channel_id=1, source_target_pairs={{0,8},{8,0},{16,24},{24,16},{32,40},{40,32},{48,56},{56,48},{64,72... | collective-permute-start | bytes 688136 | tf_op jit(solution)/shard_map/ppermute | solution.py:437
  67.8 8.7 %collective-permute-start.10 = (f32[4,56,256]{2,1,0:T(8,128)S(1)}, f32[4,56,256]{2,1,0:T(8,128)S(1)}, u32[]{:S(2)}, u32[]{:S(2)}) collective-permute-start(f32[4,56,256]{2,1,0:T(8,128)S(1)} %get-tuple-element.43), channel_id=1, source_target_pairs={{0,56},{8,16},{16,8},{24,32},{32,24},{40,48},{48,40},{56,0},{64,12... | collective-permute-start | bytes 688136 | tf_op jit(solution)/shard_map/ppermute | solution.py:438
  76.5 26.2 %all-to-all-start.3 = ((f32[8,80,128]{2,1,0:T(8,128)}), f32[8,80,128]{2,1,0:T(8,128)S(1)}, u32[]{:S(2)}, u32[]{:S(2)}) async-start(f32[8,80,128]{2,1,0:T(8,128)} %bitcast.6), calls=%async_computation.3 | async-start | bytes 655360 | tf_op jit(solution)/shard_map/all_to_all | solution.py:418
  81.6 16.9 %collective-permute-start.11 = (f32[56,512]{1,0:T(8,128)S(1)}, f32[56,512]{1,0:T(8,128)S(1)}, u32[]{:S(2)}, u32[]{:S(2)}) collective-permute-start(f32[56,512]{1,0:T(8,128)S(1)} %get-tuple-element.47), channel_id=1, source_target_pairs={{48,0},{56,8},{0,16},{8,24},{16,32},{24,40},{32,48},{40,56},{112,6... | collective-permute-start | bytes 344072 | tf_op jit(solution)/shard_map/ppermute | solution.py:442
  84.6 17.1 %collective-permute-start.12 = (f32[56,512]{1,0:T(8,128)S(1)}, f32[56,512]{1,0:T(8,128)S(1)}, u32[]{:S(2)}, u32[]{:S(2)}) collective-permute-start(f32[56,512]{1,0:T(8,128)S(1)} %get-tuple-element.48), channel_id=1, source_target_pairs={{32,0},{40,8},{48,16},{56,24},{0,32},{8,40},{16,48},{24,56},{96,64... | collective-permute-start | bytes 344072 | tf_op jit(solution)/shard_map/ppermute | solution.py:442
  88.2 13.5 %collective-permute-start.13 = (f32[56,512]{1,0:T(8,128)S(1)}, f32[56,512]{1,0:T(8,128)S(1)}, u32[]{:S(2)}, u32[]{:S(2)}) collective-permute-start(f32[56,512]{1,0:T(8,128)S(1)} %get-tuple-element.49), channel_id=1, source_target_pairs={{16,0},{24,8},{32,16},{40,24},{48,32},{56,40},{0,48},{8,56},{80,64... | collective-permute-start | bytes 344072 | tf_op jit(solution)/shard_map/ppermute | solution.py:442
  102.7 29.2 %all-to-all-start.2 = ((f32[8,56,512]{2,1,0:T(8,128)}), f32[8,56,512]{2,1,0:T(8,128)S(1)}, u32[]{:S(2)}, u32[]{:S(2)}) async-start(f32[8,56,512]{2,1,0:T(8,128)} %bitcast.4), calls=%async_computation.2 | async-start | bytes 1835008 | tf_op jit(solution)/shard_map/all_to_all | solution.py:418
  106.3 25.6 %copy-start.6 = (f32[256,512]{1,0:T(8,128)S(1)}, f32[256,512]{1,0:T(8,128)}, u32[]{:S(2)}) copy-start(f32[256,512]{1,0:T(8,128)} %copy-done.5) | copy-start | bytes 1572868
  106.3 1.9 %collective-permute-start.14 = (f32[640,128]{1,0:T(8,128)S(1)}, f32[640,128]{1,0:T(8,128)S(1)}, u32[]{:S(2)}, u32[]{:S(2)}) collective-permute-start(f32[640,128]{1,0:T(8,128)S(1)} %bitcast.11), channel_id=1, source_target_pairs={{1,0},{0,1},{3,2},{2,3},{5,4},{4,5},{7,6},{6,7},{9,8},{8,9},{11,10... | collective-permute-start | bytes 983048 | tf_op jit(solution)/shard_map/ppermute | solution.py:444
  134.5 27.4 %collective-permute-start.24 = (f16[448,512]{1,0:T(8,128)(2,1)S(1)}, f16[448,512]{1,0:T(8,128)(2,1)S(1)}, u32[]{:S(2)}, u32[]{:S(2)}) collective-permute-start(f16[448,512]{1,0:T(8,128)(2,1)S(1)} %convert_element_type.15), channel_id=1, source_target_pairs={{192,0},{200,8},{208,16},{216,24},{224,32},{232,40},{240,48},{248,... | collective-permute-start | bytes 1376264 | tf_op jit(solution)/shard_map/ppermute | solution.py:451
  135.1 26.8 %collective-permute-start.23 = (f16[448,512]{1,0:T(8,128)(2,1)S(1)}, f16[448,512]{1,0:T(8,128)(2,1)S(1)}, u32[]{:S(2)}, u32[]{:S(2)}) collective-permute-start(f16[448,512]{1,0:T(8,128)(2,1)S(1)} %convert_element_type.15), channel_id=1, source_target_pairs={{128,0},{136,8},{144,16},{152,24},{160,32},{168,40},{176,48},{184,... | collective-permute-start | bytes 1376264 | tf_op jit(solution)/shard_map/ppermute | solution.py:451
  137.2 24.7 %collective-permute-start.22 = (f16[448,512]{1,0:T(8,128)(2,1)S(1)}, f16[448,512]{1,0:T(8,128)(2,1)S(1)}, u32[]{:S(2)}, u32[]{:S(2)}) collective-permute-start(f16[448,512]{1,0:T(8,128)(2,1)S(1)} %convert_element_type.15), channel_id=1, source_target_pairs={{64,0},{72,8},{80,16},{88,24},{96,32},{104,40},{112,48},{120,56},{... | collective-permute-start | bytes 1376264 | tf_op jit(solution)/shard_map/ppermute | solution.py:451
  138.4 3.6 %collective-permute-start.17 = (f32[1,512]{1,0:T(1,128)S(1)}, f32[1,512]{1,0:T(1,128)S(1)}, u32[]{:S(2)}, u32[]{:S(2)}) collective-permute-start(f32[1,512]{1,0:T(1,128)S(1)} %get-tuple-element.53), channel_id=1, source_target_pairs={{6,0},{7,1},{0,2},{1,3},{2,4},{3,5},{4,6},{5,7},{14,8},{15,9},{8,1... | collective-permute-start | bytes 6152 | tf_op jit(solution)/shard_map/ppermute | solution.py:452
  139.6 4.6 %collective-permute-start.16 = (f32[1,512]{1,0:T(1,128)S(1)}, f32[1,512]{1,0:T(1,128)S(1)}, u32[]{:S(2)}, u32[]{:S(2)}) collective-permute-start(f32[1,512]{1,0:T(1,128)S(1)} %get-tuple-element.53), channel_id=1, source_target_pairs={{2,0},{3,1},{4,2},{5,3},{6,4},{7,5},{0,6},{1,7},{10,8},{11,9},{12,... | collective-permute-start | bytes 6152 | tf_op jit(solution)/shard_map/ppermute | solution.py:452
  142.0 5.1 %collective-permute-start.15 = (f32[1,512]{1,0:T(1,128)S(1)}, f32[1,512]{1,0:T(1,128)S(1)}, u32[]{:S(2)}, u32[]{:S(2)}) collective-permute-start(f32[1,512]{1,0:T(1,128)S(1)} %get-tuple-element.53), channel_id=1, source_target_pairs={{4,0},{5,1},{6,2},{7,3},{0,4},{1,5},{2,6},{3,7},{12,8},{13,9},{14,... | collective-permute-start | bytes 6152 | tf_op jit(solution)/shard_map/ppermute | solution.py:452
  147.1 1.5 collective-permute-start.18
  148.6 9.7 %collective-permute-start.21 = (f32[2,512]{1,0:T(2,128)S(1)}, f32[2,512]{1,0:T(2,128)S(1)}, u32[]{:S(2)}, u32[]{:S(2)}) collective-permute-start(f32[2,512]{1,0:T(2,128)S(1)} %pad_maximum_fusion.refs_4_), channel_id=1, source_target_pairs={{192,0},{200,8},{208,16},{216,24},{224,32},{232,40},{240,48},{248,... | collective-permute-start | bytes 12296 | tf_op jit(solution)/shard_map/ppermute | solution.py:456
  149.5 8.8 %collective-permute-start.20 = (f32[2,512]{1,0:T(2,128)S(1)}, f32[2,512]{1,0:T(2,128)S(1)}, u32[]{:S(2)}, u32[]{:S(2)}) collective-permute-start(f32[2,512]{1,0:T(2,128)S(1)} %pad_maximum_fusion.refs_4_), channel_id=1, source_target_pairs={{128,0},{136,8},{144,16},{152,24},{160,32},{168,40},{176,48},{184,... | collective-permute-start | bytes 12296 | tf_op jit(solution)/shard_map/ppermute | solution.py:456
  158.3 3.6 %collective-permute-start.19 = (f32[2,512]{1,0:T(2,128)S(1)}, f32[2,512]{1,0:T(2,128)S(1)}, u32[]{:S(2)}, u32[]{:S(2)}) collective-permute-start(f32[2,512]{1,0:T(2,128)S(1)} %pad_maximum_fusion.refs_4_), channel_id=1, source_target_pairs={{64,0},{72,8},{80,16},{88,24},{96,32},{104,40},{112,48},{120,56},{... | collective-permute-start | bytes 12296 | tf_op jit(solution)/shard_map/ppermute | solution.py:456
  162.0 1.5 copy-start
  162.0 1.7 %copy-start.1 = (bf16[256,1792]{1,0:T(8,128)(2,1)S(1)}, bf16[256,1792]{1,0:T(8,128)(2,1)}, u32[]{:S(2)}) copy-start(bf16[256,1792]{1,0:T(8,128)(2,1)} %gradient.3) | copy-start | bytes 2752516
  162.0 2.0 %copy-start.2 = (bf16[256,1792]{1,0:T(8,128)(2,1)S(1)}, bf16[256,1792]{1,0:T(8,128)(2,1)}, u32[]{:S(2)}) copy-start(bf16[256,1792]{1,0:T(8,128)(2,1)} %weight.1) | copy-start | bytes 2752516
